TPU v7x, 32 devices: a whole 2x2x4 slice. The times are simulated.
32 devices in a mesh: row: 4 (over y, core), col: 8 (over z, x).
Axes of the slice: x: 2, y: 2, z: 4, core: 2. Of those that a mesh axis runs over, the one named last changes fastest.
Arguments:
- layer_input: bfloat16 [256, 12288], P('col', 'row'), may hold values from -0.375 to 0.375
- weight: bfloat16 [12288, 49152], P('row', 'col'), may hold values from -0.0546875 to 0.0546875
- hidden_pre: bfloat16 [256, 49152], P('row', 'col'), may hold values from -8 to 8
- upstream: bfloat16 [256, 49152], P('row', 'col'), may hold values from -6 to 6
Outputs:
- input_grad: bfloat16 [256, 12288], P('col', 'row')
- weight_grad: bfloat16 [12288, 49152], P('row', 'col')
All inputs are finite; a program needn't handle non-finite values.
Results may differ from a plain program's by a relative error of at most 0.005.
Values may be sent and summed in bfloat16 or wider, within the bound.
No kernel may reach another device: no remote copies, remote signals or barrier semaphores. Data moves between devices by JAX's collectives and lax.ppermute only.
A program may use at most 256 MiB of HBM per device.

v0:
```python
import jax
import jax.numpy as jnp
from jax import lax
from jax.sharding import PartitionSpec as P


def gelu_slope(value):
    coeff = 0.7978845608028654
    inner = coeff * (value + 0.044715 * value * value * value)
    tanh_val = jnp.tanh(inner)
    return 0.5 * (1.0 + tanh_val) + 0.5 * value * (1.0 - tanh_val * tanh_val) * coeff * (
        1.0 + 3.0 * 0.044715 * value * value
    )


def grad_rows(hidden_rows, weight):
    return lax.dot_general(
        hidden_rows, weight, (((1,), (1,)), ((), ())), preferred_element_type=jnp.float32
    )


def outer_sum(input_rows, hidden_rows):
    return lax.dot_general(
        input_rows, hidden_rows, (((0,), (0,)), ((), ())), preferred_element_type=jnp.float32
    )


def shards(layer_input, weight, hidden_pre, upstream):
    slope = gelu_slope(hidden_pre.astype(jnp.float32))
    hidden_grad = (upstream.astype(jnp.float32) * slope).astype(jnp.bfloat16)
    gathered = lax.all_gather(layer_input, "col", axis=0, tiled=True)
    weight_sum = outer_sum(gathered, lax.all_gather(hidden_grad, "row", axis=0, tiled=True))
    terms = grad_rows(lax.all_gather(hidden_grad, "row", axis=0, tiled=True), weight)
    input_sum = lax.psum_scatter(terms, "col", scatter_dimension=0, tiled=True)
    return (input_sum.astype(jnp.bfloat16), weight_sum.astype(jnp.bfloat16))


def solution(mesh):
    in_specs = (P("col", "row"), P("row", "col"), P("row", "col"), P("row", "col"))
    out_specs = (P("col", "row"), P("row", "col"))
    return jax.shard_map(shards, mesh=mesh, in_specs=in_specs, out_specs=out_specs, check_vma=False)
```

profile of v0, /device:TPU:0, one launch (start us, length us, event | category | flops | bytes accessed | tf_op | source)
XLA Modules:
  0.0 173.5 jit_solution(17339136026476641181)
XLA Ops:
  7.2 0.0 all-gather.3.cloned.1.call-start
  7.2 3.3 %fusion.7 = bf16[64,6144]{1,0:T(8,128)(2,1)} fusion(bf16[64,6144]{1,0:T(8,128)(2,1)} %param.6, bf16[64,6144]{1,0:T(8,128)(2,1)} %param.7), kind=kLoop, calls=%fused_computation.15 | loop fusion | flops 8257536 | bytes 2359296 | tf_op jit(solution)/shard_map/convert_element_type | solution.py:30
  10.6 0.0 all-gather.3.cloned.1.call-update
  10.6 0.0 all-gather.5.cloned.1.call-start
  10.6 0.7 all-gather.5.cloned.1.call-update
  11.3 0.0 reduce-scatter.2.cloned.1.call-start
  11.4 30.6 %all-gather.3.cloned.1.call-done = bf16[256,6144]{1,0:T(8,128)(2,1)} async-done(((bf16[64,6144]{1,0:T(8,128)(2,1)}), bf16[256,6144]{1,0:T(8,128)(2,1)}) %all-gather.3.cloned.1.call-update) | async-done | bytes 3145744 | tf_op jit(solution)/shard_map/all_gather | solution.py:33
  42.0 18.8 %fusion.9 = f32[256,3072]{1,0:T(8,128)} fusion(bf16[256,6144]{1,0:T(8,128)(2,1)} %all-gather.3.cloned.1.call-done, bf16[3072,6144]{1,0:T(8,128)(2,1)} %param.5), kind=kOutput, calls=%fused_computation.17 | convolution fusion | flops 9663676416 | bytes 44040192 | tf_op jit(solution)/shard_map/dot_general | solution.py:17
  60.8 0.0 copy-start
  60.8 0.0 reduce-scatter.2.cloned.1.call-update
  60.8 27.5 %all-gather.5.cloned.1.call-done = bf16[256,3072]{1,0:T(8,128)(2,1)} async-done(((bf16[32,3072]{1,0:T(8,128)(2,1)}), bf16[256,3072]{1,0:T(8,128)(2,1)}) %all-gather.5.cloned.1.call-update) | async-done | bytes 1572880 | tf_op jit(solution)/shard_map/all_gather | solution.py:31
  88.4 0.0 copy-done
  88.4 17.5 %convert_bitcast_fusion = bf16[3072,6144]{0,1:T(8,128)(2,1)} fusion(bf16[256,6144]{1,0:T(8,128)(2,1)S(1)} %copy-done, bf16[256,3072]{1,0:T(8,128)(2,1)} %all-gather.5.cloned.1.call-done), kind=kOutput, calls=%fused_computation | convolution fusion | flops 9682550784 | bytes 42467328 | tf_op jit(solution)/shard_map/dot_general | solution.py:23
  105.9 48.7 %copy.6 = bf16[3072,6144]{1,0:T(8,128)(2,1)} copy(bf16[3072,6144]{0,1:T(8,128)(2,1)} %convert_bitcast_fusion) | data formatting | bytes 75497472
  154.6 10.7 %reduce-scatter.2.cloned.1.call-done = f32[32,3072]{1,0:T(8,128)} async-done(((f32[256,3072]{1,0:T(8,128)}), f32[32,3072]{1,0:T(8,128)}) %reduce-scatter.2.cloned.1.call-update) | async-done | bytes 393232 | tf_op jit(solution)/shard_map/reduce_scatter | solution.py:34
  165.3 1.7 convert_element_type.21
Async XLA Ops:
  7.2 34.8 %all-gather.3.cloned.1.call-start = ((), (), s32[]{:S(2)}) async-start(), calls=%async_computation.1 | async-start | bytes 3932160 | tf_op jit(solution)/shard_map/all_gather | solution.py:33
  10.6 77.8 %all-gather.5.cloned.1.call-start = ((), (), s32[]{:S(2)}) async-start(), calls=%async_computation.3 | async-start | bytes 1769472 | tf_op jit(solution)/shard_map/all_gather | solution.py:31
  11.3 153.9 %reduce-scatter.2.cloned.1.call-start = ((), (), s32[]{:S(2)}) async-start(), calls=%async_computation.2 | async-start | bytes 3538944 | tf_op jit(solution)/shard_map/reduce_scatter | solution.py:34
  60.8 27.6 %copy-start = (bf16[256,6144]{1,0:T(8,128)(2,1)S(1)}, bf16[256,6144]{1,0:T(8,128)(2,1)}, u32[]{:S(2)}) copy-start(bf16[256,6144]{1,0:T(8,128)(2,1)} %all-gather.3.cloned.1.call-done) | copy-start | bytes 9437188
Sparse Core Ops, SparseCore 0:
  10.7 31.2 all-gather.2
  44.1 44.1 all-gather.4
  92.0 73.2 reduce-scatter.1
where the time goes:
time: 175 us; the launch traced here: 174 us
  waiting for transfers between devices  69.6 us (40%)
  local copies, waits for them, and re-layouts  48.7 us (28%)
  matrix products  36.3 us (21%)
  between operations  13.7 us (8%)
  other arithmetic  5.04 us (3%)
    unnamed x3, local copies, waits for them, and re-layouts  48.7 us
    all_gather x1, waiting for transfers between devices, shards(): lax.all_gather(hidden_grad, 'row', axis=0, tiled=True)  30.6 us
    all_gather x1, waiting for transfers between devices, shards(): gathered = lax.all_gather(layer_input, 'col', axis=0, tiled=True)  27.5 us
    dot_general x1, matrix products, grad_rows(): lax.dot_general(hidden_rows, weight, (((1,), (1,)), ((), ())), preferred_...  18.8 us
    dot_general x1, matrix products, outer_sum(): lax.dot_general(input_rows, hidden_rows, (((0,), (0,)), ((), ())), prefer...  17.5 us
    reduce_scatter x1, waiting for transfers between devices, shards(): input_sum = lax.psum_scatter(terms, 'col', scatter_dimension=0, tiled=True)  10.7 us
  transfers between devices with their start and end apart: 3, of which 3 were waited for; matrix products, arithmetic and copies ran while one was open for 49% of the time, Pallas kernels for 0%

commit v1 on v0

v1 whole, which is shorter than its diff:
```python
import functools

import jax
import jax.numpy as jnp
from jax import lax
from jax.experimental import pallas as pl
from jax.experimental.pallas import tpu as pltpu
from jax.sharding import PartitionSpec as P

TERMS_SCALE = 1
OUTER_SCALE = 1


def gelu_slope(value):
    coeff = 0.7978845608028654
    inner = coeff * (value + 0.044715 * value * value * value)
    tanh_val = jnp.tanh(inner)
    return 0.5 * (1.0 + tanh_val) + 0.5 * value * (1.0 - tanh_val * tanh_val) * coeff * (
        1.0 + 3.0 * 0.044715 * value * value
    )


def hidden_grad_of(pre, upstream):
    return (upstream.astype(jnp.float32) * gelu_slope(pre.astype(jnp.float32))).astype(jnp.bfloat16)


def grad_rows(hidden_rows, weight):
    return lax.dot_general(
        hidden_rows, weight, (((1,), (1,)), ((), ())), preferred_element_type=jnp.float32
    )


def outer_sum(input_rows, hidden_rows):
    return lax.dot_general(
        input_rows, hidden_rows, (((0,), (0,)), ((), ())), preferred_element_type=jnp.float32
    )


def general_shards(layer_input, weight, hidden_pre, upstream):
    hidden_grad = hidden_grad_of(hidden_pre, upstream)
    hidden_all = lax.all_gather(hidden_grad, "row", axis=0, tiled=True)
    input_all = lax.all_gather(layer_input, "col", axis=0, tiled=True)
    terms = grad_rows(hidden_all, weight)
    input_sum = lax.psum_scatter(terms, "col", scatter_dimension=0, tiled=True)
    weight_sum = outer_sum(input_all, hidden_all)
    return (input_sum.astype(jnp.bfloat16), weight_sum.astype(jnp.bfloat16))


def slope_columns(pre, up, start, size, out):
    step = 512

    @pl.loop(0, size // step)
    def _(i):
        here = pl.ds(pl.multiple_of(start + i * step, step), step)
        out[:, pl.ds(pl.multiple_of(i * step, step), step)] = hidden_grad_of(pre[:, here], up[:, here])


def first_hidden_kernel(size, pre_hbm, up_hbm, pre, up, out, sems):
    copies = []
    for n, cols in enumerate((pl.ds(0, size), pl.ds(size, pre.shape[1] - size))):
        for m, (source, target) in enumerate(((pre_hbm, pre), (up_hbm, up))):
            copies.append(pltpu.make_async_copy(source.at[:, cols], target.at[:, cols], sems.at[n, m]))
            copies[-1].start()
    copies[0].wait()
    copies[1].wait()
    slope_columns(pre, up, 0, size, out)
    copies[2].wait()
    copies[3].wait()


def first_hidden(pre, up, size):
    rows, width = pre.shape
    vmem, hbm = pl.BlockSpec(memory_space=pltpu.VMEM), pl.BlockSpec(memory_space=pl.ANY)
    return pl.pallas_call(
        functools.partial(first_hidden_kernel, size),
        in_specs=[hbm] * 2,
        out_specs=[vmem] * 3,
        out_shape=[pltpu.VMEM(shape, jnp.bfloat16) for shape in ((rows, width), (rows, width), (rows, size))],
        scratch_shapes=[pltpu.SemaphoreType.DMA((2, 2))],
        compiler_params=pltpu.CompilerParams(vmem_limit_bytes=8 << 20),
        cost_estimate=pl.CostEstimate(flops=0, bytes_accessed=4 * pre.size, transcendentals=0),
        name="first_hidden",
    )(pre, up)


def next_hidden_kernel(start, size, pre, up, before, out):
    slope_columns(pre, up, start, size, out)


def next_hidden(pre, up, before, start, size):
    rows = pre.shape[0]
    vmem, hbm = pl.BlockSpec(memory_space=pltpu.VMEM), pl.BlockSpec(memory_space=pl.ANY)
    return pl.pallas_call(
        functools.partial(next_hidden_kernel, start, size),
        in_specs=[vmem, vmem, hbm],
        out_specs=vmem,
        out_shape=pltpu.VMEM((rows, size), jnp.bfloat16),
        compiler_params=pltpu.CompilerParams(vmem_limit_bytes=8 << 20),
        cost_estimate=pl.CostEstimate(flops=0, bytes_accessed=rows * size, transcendentals=0),
        name="next_hidden",
    )(pre, up, before)


def joined_kernel(*refs):
    parts, out = refs[:-1], refs[-1]
    start = 0
    for part in parts:
        out[:, pl.ds(start, part.shape[1])] = part[...]
        start += part.shape[1]


def joined(parts):
    rows, width = parts[0].shape[0], sum(part.shape[1] for part in parts)
    vmem = pl.BlockSpec(memory_space=pltpu.VMEM)
    return pl.pallas_call(
        joined_kernel,
        in_specs=[vmem] * len(parts),
        out_specs=vmem,
        out_shape=pltpu.VMEM((rows, width), jnp.bfloat16),
        compiler_params=pltpu.CompilerParams(vmem_limit_bytes=8 << 20),
        cost_estimate=pl.CostEstimate(flops=0, bytes_accessed=rows * width, transcendentals=0),
        name="joined",
    )(*parts)


def weight_copies(weight_ref, tiles, sems, start, size, count):
    rows = weight_ref.shape[0] // count
    return [
        pltpu.make_async_copy(
            weight_ref.at[pl.ds(n * rows, rows), pl.ds(start, size)], tiles.at[pl.ds(n * rows, rows)], sems.at[n]
        )
        for n in range(count)
    ]


COPIES = 6


def load_kernel(start, size, weight_ref, input_ref, after_ref, tiles, input_copy, sems):
    copies = weight_copies(weight_ref, tiles, sems, start, size, COPIES)
    copies.append(pltpu.make_async_copy(input_ref, input_copy, sems.at[COPIES]))
    for copy in copies:
        copy.start()
    for copy in copies:
        copy.wait()


def load_part(weight, layer_input, after, start, size):
    model = weight.shape[0]
    hbm = pl.BlockSpec(memory_space=pl.ANY)
    return pl.pallas_call(
        functools.partial(load_kernel, start, size),
        in_specs=[hbm] * 3,
        out_specs=[pl.BlockSpec(memory_space=pltpu.VMEM)] * 2,
        out_shape=[pltpu.VMEM((model, size), jnp.bfloat16), pltpu.VMEM(layer_input.shape, jnp.bfloat16)],
        scratch_shapes=[pltpu.SemaphoreType.DMA((COPIES + 1,))],
        compiler_params=pltpu.CompilerParams(vmem_limit_bytes=16 << 20),
        cost_estimate=pl.CostEstimate(flops=0, bytes_accessed=2 * size * model, transcendentals=0),
        name="weight_load",
    )(weight, layer_input, after)


def gather_hidden(place_ref, own, sib, far, start, hidden):
    _, rows, size = far.shape
    cols, core = pl.ds(start, size), place_ref[3]
    for j, part in enumerate((own.at[:, cols], sib.at[:, cols], far.at[core], far.at[1 - core])):
        hidden[pl.ds(rows * j, rows)] = part[...]


def terms_kernel(starts, sizes, n, block, place_ref, own, sib, far, tiles, *refs):
    first, last = n == 0, n == len(sizes) - 1
    refs = list(refs)
    held = None if first else refs.pop(0)
    weight = None if last else refs.pop(0)
    if last:
        sends, keeps, refs = refs[:4], refs[4:8], refs[8:]
        total, hidden = refs
    else:
        total, later, hidden, sems = refs
        copies = weight_copies(weight, later, sems, starts[n + 1], sizes[n + 1], COPIES)
        for copy in copies:
            copy.start()
    gather_hidden(place_ref, own, sib, far, starts[n], hidden)
    rows, model = far.shape[1], tiles.shape[0]

    @pl.loop(0, model // block)
    def _(i):
        here = pl.ds(pl.multiple_of(i * block, block), block)
        term = grad_rows(hidden[...], tiles[here]).reshape(8, rows // 2, block)
        if not first:
            term = term + held[:, :, here]
        total[:, :, here] = term

    if last:
        row, z, x = place_ref[0], place_ref[1], place_ref[2]
        for k in range(4):
            slot = 2 * (row ^ z ^ k)
            sends[k][...] = total[slot + (1 - x)].astype(jnp.bfloat16)
            keeps[k][...] = total[slot + x]
    else:
        for copy in copies:
            copy.wait()


def terms_part(place, parts, tiles, held, weight, starts, sizes, n):
    _, rows, size = parts[2].shape
    model = weight.shape[0]
    block = 1024
    vmem, hbm = pl.BlockSpec(memory_space=pltpu.VMEM), pl.BlockSpec(memory_space=pl.ANY)
    first, last = n == 0, n == len(sizes) - 1
    half = rows // 2
    operands = [place, *parts, tiles]
    in_specs = [pl.BlockSpec(memory_space=pltpu.SMEM)] + [vmem] * 4
    aliases = {}
    if not first:
        if not last:
            aliases = {len(operands): 0}
        operands.append(held)
        in_specs.append(vmem)
    if not last:
        operands.append(weight)
        in_specs.append(hbm)
    scratch = [pltpu.VMEM((4 * rows, size), jnp.bfloat16)]
    if last:
        scratch = [pltpu.VMEM((8, half, model), jnp.float32)] + scratch
        out_shape = [pltpu.VMEM((half, model), jnp.bfloat16)] * 4
        out_shape += [pltpu.VMEM((half, model), jnp.float32)] * 4
    else:
        scratch.append(pltpu.SemaphoreType.DMA((COPIES,)))
        out_shape = [
            pltpu.VMEM((8, half, model), jnp.float32),
            pltpu.VMEM((model, sizes[n + 1]), jnp.bfloat16),
        ]
    return pl.pallas_call(
        functools.partial(terms_kernel, starts, sizes, n, block),
        in_specs=in_specs,
        out_specs=[vmem] * len(out_shape),
        out_shape=out_shape,
        scratch_shapes=scratch,
        input_output_aliases=aliases,
        compiler_params=pltpu.CompilerParams(vmem_limit_bytes=16 << 20),
        cost_estimate=pl.CostEstimate(flops=8 * rows * size * model, bytes_accessed=TERMS_SCALE * 2 * size * model, transcendentals=0),
        name="terms",
    )(*operands)


def input_kernel(place_ref, *refs):
    blocks, out, held = refs[:8], refs[8], refs[9]
    row, z, x = place_ref[0], place_ref[1], place_ref[2]
    half = blocks[0].shape[0]
    for k in range(4):
        for i in range(2):
            held[2 * (row ^ z ^ k) + (x ^ i)] = blocks[2 * k + i][...]
    out[...] = held[...].reshape(8 * half, -1).T


def input_columns(place, blocks):
    half, model = blocks[0].shape
    vmem = pl.BlockSpec(memory_space=pltpu.VMEM)
    return pl.pallas_call(
        input_kernel,
        in_specs=[pl.BlockSpec(memory_space=pltpu.SMEM)] + [vmem] * 8,
        out_specs=vmem,
        out_shape=pltpu.VMEM((model, 8 * half), jnp.bfloat16),
        scratch_shapes=[pltpu.VMEM((8, half, model), jnp.bfloat16)],
        compiler_params=pltpu.CompilerParams(vmem_limit_bytes=16 << 20),
        cost_estimate=pl.CostEstimate(flops=0, bytes_accessed=32 * half * model, transcendentals=0),
        name="input_columns",
    )(place, *blocks)


def outer_kernel(start, size, block, first, place_ref, columns_ref, own, sib, far, *refs):
    out, hidden, tiles, sems = refs if first else refs[1:]
    gather_hidden(place_ref, own, sib, far, start, hidden)
    slots = tiles.shape[0]
    copies = []
    for n in range(size // block):
        slot = n % slots
        if n >= slots:
            copies[n - slots].wait()
        tiles[slot] = jnp.dot(
            columns_ref[...], hidden[:, pl.ds(n * block, block)], preferred_element_type=jnp.float32
        ).astype(jnp.bfloat16)
        copies.append(
            pltpu.make_async_copy(tiles.at[slot], out.at[:, pl.ds(start + n * block, block)], sems.at[slot])
        )
        copies[-1].start()
    for copy in copies[-slots:]:
        copy.wait()


def outer_part(place, columns, parts, held, start, whole):
    _, rows, size = parts[2].shape
    model, tokens = columns.shape
    block = 512
    first = held is None
    vmem, hbm = pl.BlockSpec(memory_space=pltpu.VMEM), pl.BlockSpec(memory_space=pl.ANY)
    operands = [place, columns, *parts] + ([] if first else [held])
    slots = min(3, size // block)
    return pl.pallas_call(
        functools.partial(outer_kernel, start, size, block, first),
        in_specs=[pl.BlockSpec(memory_space=pltpu.SMEM)] + [vmem] * 4 + ([] if first else [hbm]),
        out_specs=hbm,
        out_shape=jax.ShapeDtypeStruct((model, whole), jnp.bfloat16),
        scratch_shapes=[
            pltpu.VMEM((tokens, size), jnp.bfloat16),
            pltpu.VMEM((slots, model, block), jnp.bfloat16),
            pltpu.SemaphoreType.DMA((slots,)),
        ],
        input_output_aliases={} if first else {5: 0},
        compiler_params=pltpu.CompilerParams(vmem_limit_bytes=16 << 20),
        cost_estimate=pl.CostEstimate(
            flops=2 * tokens * size * model, bytes_accessed=OUTER_SCALE * 2 * size * model, transcendentals=0
        ),
        name="outer",
    )(*operands)


def fenced(value, other):
    return lax.optimization_barrier((value, other))[0]


def swap(value, axis, size, bits):
    return lax.ppermute(value, axis, [(n, n ^ bits) for n in range(size)])


def paired_shards(layer_input, weight, hidden_pre, upstream):
    hidden = hidden_pre.shape[1]
    parts = 3
    sizes = [hidden // parts] * parts
    starts = [sum(sizes[:n]) for n in range(parts)]
    row, col = lax.axis_index("row"), lax.axis_index("col")
    place = jnp.stack([row, col // 2, col % 2, row % 2]).astype(jnp.int32)

    across = functools.partial(swap, axis="col", size=8)
    along = functools.partial(swap, axis="row", size=4)

    pre, up, part = first_hidden(hidden_pre, upstream, sizes[0])
    sent = [part]
    for n in range(1, parts):
        sent.append(next_hidden(pre, up, sent[-1], starts[n], sizes[n]))
    far = [along(sent[0], bits=2)]
    own = joined(sent)
    sib = along(own, bits=1)

    far.append(along(fenced(sent[1], sib), bits=2))
    early = fenced(layer_input, sib)
    lines = [layer_input, None, across(early, bits=4), across(early, bits=6)]
    crossed = [across(early, bits=1)]
    tiles, _ = load_part(weight, layer_input, sib, starts[0], sizes[0])
    far.append(along(fenced(sent[2], tiles), bits=2))
    tiles = fenced(tiles, crossed[0])

    pairs, held = [], None
    for n in range(parts):
        far[n], tiles, held = lax.optimization_barrier((far[n], tiles, held))
        pairs.append(lax.all_gather(far[n], "row", axis=0, axis_index_groups=[[0, 1], [2, 3]]))
        out = terms_part(place, [own, sib, pairs[n]], tiles, held, weight, starts, sizes, n)
        if n < parts - 1:
            held, tiles = out
        if n == 0:
            lines[1] = across(fenced(layer_input, tiles), bits=2)
            crossed.append(across(fenced(lines[3], tiles), bits=1))
        if n == 1:
            for k in (2, 1):
                crossed.append(across(fenced(lines[k], tiles), bits=1))
    sends, keeps = out[:4], out[4:]
    blocks = []
    for k, n in enumerate((0, 3, 2, 1)):
        blocks += [lines[k], crossed[n]]

    order = (2, 3, 1, 0)
    got = {k: across(sends[k], bits=1) for k in order}
    columns = input_columns(place, blocks)
    weight_grad, ends, pair = None, {}, {}
    for n, k in enumerate(order):
        if n < parts:
            weight_grad = outer_part(place, columns, [own, sib, pairs[n]], weight_grad, starts[n], hidden)
        if k:
            got[k], weight_grad = lax.optimization_barrier((got[k], weight_grad))
        pair[k] = keeps[k] + got[k].astype(jnp.float32)
        if k:
            rounded = pair[k].astype(jnp.bfloat16)
            rounded, columns = lax.optimization_barrier((rounded, columns))
            ends[k] = across(rounded, bits=2 * k)
    input_sum = pair[0]
    for n, k in enumerate(order[:3]):
        input_sum = input_sum + ends[k].astype(jnp.float32)
        if n < 2:
            input_sum, ends[order[n + 1]] = lax.optimization_barrier((input_sum, ends[order[n + 1]]))
    return (input_sum.astype(jnp.bfloat16), weight_grad)


def solution(mesh):
    in_specs = (P("col", "row"), P("row", "col"), P("row", "col"), P("row", "col"))
    out_specs = (P("col", "row"), P("row", "col"))
    paired = mesh.shape["row"] == 4 and mesh.shape["col"] == 8
    shards = paired_shards if paired else general_shards
    return jax.shard_map(shards, mesh=mesh, in_specs=in_specs, out_specs=out_specs, check_vma=False)
```

time: 175 us -> 83.7 us (0.48)
  waiting for transfers between devices: 69.6 us -> 7.75 us
  local copies, waits for them, and re-layouts: 48.7 us -> 3.22 us
  Pallas kernels: 0 us -> 42 us
  matrix products: 36.3 us -> 0 us
  starting transfers between devices: 0.12 us -> 22.1 us
  between operations: 13.7 us -> 0.83 us
  blocking collectives: 0 us -> 6.51 us
  other arithmetic: 5.04 us -> 1.04 us
    all_gather x2 -> x0, waiting for transfers between devices: 58.1 us -> none  [the longest x1 30.6 us: shards(): lax.all_gather(hidden_grad, 'row', axis=0, tiled=True)]
    unnamed x3 -> x8, local copies, waits for them, and re-layouts: 48.7 us -> 3.22 us
    pallas_call x0 -> x12, Pallas kernels: none -> 42 us  [the longest x3 18.7 us: outer_part(): pl.pallas_call(functools.partial(outer_kernel, start, size, block, first)...]
    dot_general x2 -> x0, matrix products: 36.3 us -> none  [the longest x1 18.8 us: grad_rows(): lax.dot_general(hidden_rows, weight, (((1,), (1,)), ((), ())), preferred_...]
    ppermute x0 -> x18, starting transfers between devices: none -> 22.1 us  [swap(): return lax.ppermute(value, axis, [(n, n ^ bits) for n in range(size)])]
    reduce_scatter x1 -> x0, waiting for transfers between devices: 10.7 us -> none  [shards(): input_sum = lax.psum_scatter(terms, 'col', scatter_dimension=0, tiled=True)]
    ppermute x0 -> x18, waiting for transfers between devices: none -> 7.75 us  [swap(): return lax.ppermute(value, axis, [(n, n ^ bits) for n in range(size)])]
    all_gather x0 -> x3, blocking collectives: none -> 6.51 us  [paired_shards(): lax.all_gather(far[n], 'row', axis=0, axis_index_groups=[[0, 1], [2, 3]])]
  transfers between devices with their start and end apart: 3 -> 18, of which waited for: 3 -> 2; matrix products, arithmetic and copies ran while one was open for 49% -> 0% of each run, Pallas kernels for 0% -> 49%
where the time goes in v1:
time: 83.7 us; the launch traced here: 83.5 us
  Pallas kernels  42 us (50%)
  starting transfers between devices  22.1 us (26%)
  waiting for transfers between devices  7.75 us (9%)
  blocking collectives  6.51 us (8%)
  local copies, waits for them, and re-layouts  3.22 us (4%)
  other arithmetic  1.04 us (1%)
    ppermute x18, starting transfers between devices, swap(): return lax.ppermute(value, axis, [(n, n ^ bits) for n in range(size)])  22.1 us
    pallas_call x3, Pallas kernels, outer_part(): pl.pallas_call(functools.partial(outer_kernel, start, size, block, first)...  18.7 us
    pallas_call x3, Pallas kernels, terms_part(): pl.pallas_call(functools.partial(terms_kernel, starts, sizes, n, block),...  15.4 us
    ppermute x18, waiting for transfers between devices, swap(): return lax.ppermute(value, axis, [(n, n ^ bits) for n in range(size)])  7.75 us
    all_gather x3, blocking collectives, paired_shards(): lax.all_gather(far[n], 'row', axis=0, axis_index_groups=[[0, 1], [2, 3]])  6.51 us
    pallas_call x1, Pallas kernels, load_part(): pl.pallas_call(functools.partial(load_kernel, start, size), in_specs=[hbm...  5.42 us
    unnamed x8, local copies, waits for them, and re-layouts  3.22 us
  transfers between devices with their start and end apart: 18, of which 2 were waited for; matrix products, arithmetic and copies ran while one was open for 0% of the time, Pallas kernels for 49%

profile of v1, /device:TPU:0, one launch (start us, length us, event | category | flops | bytes accessed | tf_op | source)
XLA Modules:
  0.0 83.5 jit_solution(5197403551757007165)
XLA Ops:
  0.6 1.1 %copy-done.2 = bf16[64,6144]{1,0:T(8,128)(2,1)S(1)} copy-done((bf16[64,6144]{1,0:T(8,128)(2,1)S(1)}, bf16[64,6144]{1,0:T(8,128)(2,1)}, u32[]{:S(2)}) %copy-start.2) | copy-done | bytes 786456
  1.8 1.1 %copy-done.3 = bf16[64,6144]{1,0:T(8,128)(2,1)S(1)} copy-done((bf16[64,6144]{1,0:T(8,128)(2,1)S(1)}, bf16[64,6144]{1,0:T(8,128)(2,1)}, u32[]{:S(2)}) %copy-start.3) | copy-done | bytes 786456
  4.9 2.6 %collective-permute-start.3 = (bf16[64,2048]{1,0:T(8,128)(2,1)S(1)}, bf16[64,2048]{1,0:T(8,128)(2,1)S(1)}, u32[]{:S(2)}, u32[]{:S(2)}) collective-permute-start(bf16[64,2048]{1,0:T(8,128)(2,1)S(1)} %get-tuple-element.49.before.refs_0_), channel_id=1, source_target_pairs={{0,16},{8,24},{16,0},{24,8},{1,17},{9,25},{17,1},{25,9},{2,18},{10... | collective-permute-start | bytes 786440 | tf_op jit(solution)/shard_map/ppermute | solution.py:324
  7.5 2.2 %collective-permute-start.4 = (bf16[32,3072]{1,0:T(8,128)(2,1)}, bf16[32,3072]{1,0:T(8,128)(2,1)S(1)}, u32[]{:S(2)}, u32[]{:S(2)}) collective-permute-start(bf16[32,3072]{1,0:T(8,128)(2,1)} %refs_0_.3), channel_id=1, source_target_pairs={{0,1},{1,0},{2,3},{3,2},{4,5},{5,4},{6,7},{7,6},{8,9},{9,8},{10,11... | collective-permute-start | bytes 589832 | tf_op jit(solution)/shard_map/ppermute | solution.py:324
  9.7 2.6 %collective-permute-start.9 = (bf16[32,3072]{1,0:T(8,128)(2,1)}, bf16[32,3072]{1,0:T(8,128)(2,1)S(1)}, u32[]{:S(2)}, u32[]{:S(2)}) collective-permute-start(bf16[32,3072]{1,0:T(8,128)(2,1)} %refs_0_.3), channel_id=1, source_target_pairs={{0,4},{1,5},{2,6},{3,7},{4,0},{5,1},{6,2},{7,3},{8,12},{9,13},{10,... | collective-permute-start | bytes 589832 | tf_op jit(solution)/shard_map/ppermute | solution.py:324
  12.3 1.3 %collective-permute-start.11 = (bf16[32,3072]{1,0:T(8,128)(2,1)}, bf16[32,3072]{1,0:T(8,128)(2,1)S(1)}, u32[]{:S(2)}, u32[]{:S(2)}) collective-permute-start(bf16[32,3072]{1,0:T(8,128)(2,1)} %refs_0_.3), channel_id=1, source_target_pairs={{0,6},{1,7},{2,4},{3,5},{4,2},{5,3},{6,0},{7,1},{8,14},{9,15},{10,... | collective-permute-start | bytes 589832 | tf_op jit(solution)/shard_map/ppermute | solution.py:324
  14.6 5.4 %weight_load.1 = (bf16[3072,2048]{1,0:T(8,128)(2,1)S(1)}, bf16[32,3072]{1,0:T(8,128)(2,1)}) custom-call(bf16[3072,6144]{1,0:T(8,128)(2,1)} %refs_1_.1, bf16[32,3072]{1,0:T(8,128)(2,1)S(1)} %copy-done, bf16[64,6144]{1,0:T(8,128)(2,1)S(1)} %collective-permute-done.after_ref.sib), custom_call_target="tpu_custom_call" | custom-call | bytes 12582912 | tf_op jit(solution)/shard_map/weight_load/pallas_call | solution.py:151
  20.0 1.6 %collective-permute-start.1 = (bf16[64,2048]{1,0:T(8,128)(2,1)S(1)}, bf16[64,2048]{1,0:T(8,128)(2,1)S(1)}, u32[]{:S(2)}, u32[]{:S(2)}) collective-permute-start(bf16[64,2048]{1,0:T(8,128)(2,1)S(1)} %next_hidden.3.refs_2_), channel_id=1, source_target_pairs={{0,16},{8,24},{16,0},{24,8},{1,17},{9,25},{17,1},{25,9},{2,18},{10... | collective-permute-start | bytes 786440 | tf_op jit(solution)/shard_map/ppermute | solution.py:324
  22.1 2.2 %all-gather = bf16[128,2048]{1,0:T(8,128)(2,1)S(1)} all-gather(bf16[64,2048]{1,0:T(8,128)(2,1)S(1)} %collective-permute-done.3), channel_id=2, replica_groups={{0,8},{16,24},{1,9},{17,25},{2,10},{18,26},{3,11},{19,27},{4,12},{20,28..., dimensions={0}, use_global_device_ids=true | all-gather | bytes 786432 | tf_op jit(solution)/shard_map/all_gather | solution.py:357
  24.3 5.3 %terms.3 = (f32[8,32,3072]{2,1,0:T(8,128)S(1)}, bf16[3072,2048]{1,0:T(8,128)(2,1)S(1)}) custom-call(s32[4]{0:T(128)S(1)} %pad_add_fusion.place_ref, bf16[64,6144]{1,0:T(8,128)(2,1)S(1)} %joined.1.own, bf16[64,6144]{1,0:T(8,128)(2,1)S(1)} %collective-permute-done.after_ref.sib, bf16[2,64,2048]{2,1,0:T(8,128)(2,1)S(1)} %bitcast.7, ...), custom_call_target="tpu_custom_call" | custom-call | flops 3221225472 | bytes 12582912 | tf_op jit(solution)/shard_map/terms/pallas_call | solution.py:234
  30.5 2.8 %collective-permute-done.2 = bf16[64,2048]{1,0:T(8,128)(2,1)S(1)} collective-permute-done((bf16[64,2048]{1,0:T(8,128)(2,1)S(1)}, bf16[64,2048]{1,0:T(8,128)(2,1)S(1)}, u32[]{:S(2)}, u32[]{:S(2)}) %collective-permute-start.2) | collective-permute-done | bytes 262176 | tf_op jit(solution)/shard_map/ppermute | solution.py:324
  33.3 2.2 %all-gather.1 = bf16[128,2048]{1,0:T(8,128)(2,1)S(1)} all-gather(bf16[64,2048]{1,0:T(8,128)(2,1)S(1)} %collective-permute-done.2), channel_id=3, replica_groups={{0,8},{16,24},{1,9},{17,25},{2,10},{18,26},{3,11},{19,27},{4,12},{20,28..., dimensions={0}, use_global_device_ids=true | all-gather | bytes 786432 | tf_op jit(solution)/shard_map/all_gather | solution.py:357
  35.4 5.3 %terms.4 = (f32[8,32,3072]{2,1,0:T(8,128)S(1)}, bf16[3072,2048]{1,0:T(8,128)(2,1)S(1)}) custom-call(s32[4]{0:T(128)S(1)} %pad_add_fusion.place_ref, bf16[64,6144]{1,0:T(8,128)(2,1)S(1)} %joined.1.own, bf16[64,6144]{1,0:T(8,128)(2,1)S(1)} %collective-permute-done.after_ref.sib, bf16[2,64,2048]{2,1,0:T(8,128)(2,1)S(1)} %bitcast.9, ...), custom_call_target="tpu_custom_call", output_to_operand_aliasing={{0}: (5, {})} | custom-call | flops 3221225472 | bytes 12582912 | tf_op jit(solution)/shard_map/terms/pallas_call | solution.py:234
  41.3 2.2 %all-gather.2 = bf16[128,2048]{1,0:T(8,128)(2,1)S(1)} all-gather(bf16[64,2048]{1,0:T(8,128)(2,1)S(1)} %collective-permute-done.1), channel_id=4, replica_groups={{0,8},{16,24},{1,9},{17,25},{2,10},{18,26},{3,11},{19,27},{4,12},{20,28..., dimensions={0}, use_global_device_ids=true | all-gather | bytes 786432 | tf_op jit(solution)/shard_map/all_gather | solution.py:357
  43.5 1.5 %collective-permute-start.8 = (bf16[32,3072]{1,0:T(8,128)(2,1)S(1)}, bf16[32,3072]{1,0:T(8,128)(2,1)S(1)}, u32[]{:S(2)}, u32[]{:S(2)}) collective-permute-start(bf16[32,3072]{1,0:T(8,128)(2,1)S(1)} %collective-permute-done.7.refs_2_), channel_id=1, source_target_pairs={{0,1},{1,0},{2,3},{3,2},{4,5},{5,4},{6,7},{7,6},{8,9},{9,8},{10,11... | collective-permute-start | bytes 589832 | tf_op jit(solution)/shard_map/ppermute | solution.py:324
  45.0 4.8 %terms.5 = (bf16[32,3072]{1,0:T(8,128)(2,1)S(1)}, bf16[32,3072]{1,0:T(8,128)(2,1)S(1)}, bf16[32,3072]{1,0:T(8,128)(2,1)S(1)}, bf16[32,3072]{1,0:T(8,128)(2,1)S(1...) custom-call(s32[4]{0:T(128)S(1)} %pad_add_fusion.place_ref, ...), custom_call_target="tpu_custom_call" | custom-call | flops 3221225472 | bytes 12582912 | tf_op jit(solution)/shard_map/terms/pallas_call | solution.py:234
  50.4 1.5 %collective-permute-start.5 = (bf16[32,3072]{1,0:T(8,128)(2,1)S(1)}, bf16[32,3072]{1,0:T(8,128)(2,1)S(1)}, u32[]{:S(2)}, u32[]{:S(2)}) collective-permute-start(bf16[32,3072]{1,0:T(8,128)(2,1)S(1)} %get-tuple-element.70), channel_id=1, source_target_pairs={{0,1},{1,0},{2,3},{3,2},{4,5},{5,4},{6,7},{7,6},{8,9},{9,8},{10,11... | collective-permute-start | bytes 589832 | tf_op jit(solution)/shard_map/ppermute | solution.py:324
  52.5 1.5 %collective-permute-start.16 = (bf16[32,3072]{1,0:T(8,128)(2,1)S(1)}, bf16[32,3072]{1,0:T(8,128)(2,1)S(1)}, u32[]{:S(2)}, u32[]{:S(2)}) collective-permute-start(bf16[32,3072]{1,0:T(8,128)(2,1)S(1)} %get-tuple-element.88), channel_id=1, source_target_pairs={{0,1},{1,0},{2,3},{3,2},{4,5},{5,4},{6,7},{7,6},{8,9},{9,8},{10,11... | collective-permute-start | bytes 589832 | tf_op jit(solution)/shard_map/ppermute | solution.py:324
  55.1 6.2 %outer.3.refs_0_ = bf16[3072,6144]{1,0:T(8,128)(2,1)} custom-call(s32[4]{0:T(128)S(1)} %pad_add_fusion.place_ref, bf16[3072,256]{1,0:T(8,128)(2,1)S(1)} %input_columns.1.columns_ref, bf16[64,6144]{1,0:T(8,128)(2,1)S(1)} %joined.1.own, bf16[64,6144]{1,0:T(8,128)(2,1)S(1)} %collective-permute-done.after_ref.sib, bf16[2,64,2048]{2,1,0:T(8,128)(2,1)S(1)} %bitcast.8), custom_call_target="tpu_custom_call" | custom-call | flops 3221225472 | bytes 12582912 | tf_op jit(solution)/shard_map/outer/pallas_call | solution.py:300
  61.4 1.7 %collective-permute-start.13 = (bf16[32,3072]{1,0:T(8,128)(2,1)S(1)}, bf16[32,3072]{1,0:T(8,128)(2,1)S(1)}, u32[]{:S(2)}, u32[]{:S(2)}) collective-permute-start(bf16[32,3072]{1,0:T(8,128)(2,1)S(1)} %add_convert_fusion.3), channel_id=1, source_target_pairs={{0,4},{1,5},{2,6},{3,7},{4,0},{5,1},{6,2},{7,3},{8,12},{9,13},{10,... | collective-permute-start | bytes 589832 | tf_op jit(solution)/shard_map/ppermute | solution.py:324
  63.1 6.2 %outer.4.refs_0_ = bf16[3072,6144]{1,0:T(8,128)(2,1)} custom-call(s32[4]{0:T(128)S(1)} %pad_add_fusion.place_ref, bf16[3072,256]{1,0:T(8,128)(2,1)S(1)} %input_columns.1.columns_ref, bf16[64,6144]{1,0:T(8,128)(2,1)S(1)} %joined.1.own, bf16[64,6144]{1,0:T(8,128)(2,1)S(1)} %collective-permute-done.after_ref.sib, ...), custom_call_target="tpu_custom_call", output_to_operand_aliasing={{}: (5, {})} | custom-call | flops 3221225472 | bytes 12582912 | tf_op jit(solution)/shard_map/outer/pallas_call | solution.py:300
  69.4 1.3 %collective-permute-start.15 = (bf16[32,3072]{1,0:T(8,128)(2,1)S(1)}, bf16[32,3072]{1,0:T(8,128)(2,1)S(1)}, u32[]{:S(2)}, u32[]{:S(2)}) collective-permute-start(bf16[32,3072]{1,0:T(8,128)(2,1)S(1)} %add_convert_fusion.2), channel_id=1, source_target_pairs={{0,6},{1,7},{2,4},{3,5},{4,2},{5,3},{6,0},{7,1},{8,14},{9,15},{10,... | collective-permute-start | bytes 589832 | tf_op jit(solution)/shard_map/ppermute | solution.py:324
  70.7 6.2 %outer.5 = bf16[3072,6144]{1,0:T(8,128)(2,1)} custom-call(s32[4]{0:T(128)S(1)} %pad_add_fusion.place_ref, bf16[3072,256]{1,0:T(8,128)(2,1)S(1)} %input_columns.1.columns_ref, bf16[64,6144]{1,0:T(8,128)(2,1)S(1)} %joined.1.own, bf16[64,6144]{1,0:T(8,128)(2,1)S(1)} %collective-permute-done.after_ref.sib, ...), custom_call_target="tpu_custom_call", output_to_operand_aliasing={{}: (5, {})} | custom-call | flops 3221225472 | bytes 12582912 | tf_op jit(solution)/shard_map/outer/pallas_call | solution.py:300
  77.8 4.9 %collective-permute-done.17 = bf16[32,3072]{1,0:T(8,128)(2,1)S(1)} collective-permute-done((bf16[32,3072]{1,0:T(8,128)(2,1)S(1)}, bf16[32,3072]{1,0:T(8,128)(2,1)S(1)}, u32[]{:S(2)}, u32[]{:S(2)}) %collective-permute-start.17) | collective-permute-done | bytes 196640 | tf_op jit(solution)/shard_map/ppermute | solution.py:324
  (42 shorter events, 8.9 us)
Async XLA Ops:
  0.6 1.1 %copy-start.2 = (bf16[64,6144]{1,0:T(8,128)(2,1)S(1)}, bf16[64,6144]{1,0:T(8,128)(2,1)}, u32[]{:S(2)}) copy-start(bf16[64,6144]{1,0:T(8,128)(2,1)} %pre_hbm.1) | copy-start | bytes 2359300
  1.8 1.1 %copy-start.3 = (bf16[64,6144]{1,0:T(8,128)(2,1)S(1)}, bf16[64,6144]{1,0:T(8,128)(2,1)}, u32[]{:S(2)}) copy-start(bf16[64,6144]{1,0:T(8,128)(2,1)} %up_hbm.1) | copy-start | bytes 2359300
  4.3 3.1 %collective-permute-start = (bf16[64,6144]{1,0:T(8,128)(2,1)S(1)}, bf16[64,6144]{1,0:T(8,128)(2,1)S(1)}, u32[]{:S(2)}, u32[]{:S(2)}) collective-permute-start(bf16[64,6144]{1,0:T(8,128)(2,1)S(1)} %joined.1.own), channel_id=1, source_target_pairs={{0,8},{8,0},{16,24},{24,16},{1,9},{9,1},{17,25},{25,17},{2,10},{10... | collective-permute-start | bytes 2359304 | tf_op jit(solution)/shard_map/ppermute | solution.py:324
  4.9 17.3 %collective-permute-start.3 = (bf16[64,2048]{1,0:T(8,128)(2,1)S(1)}, bf16[64,2048]{1,0:T(8,128)(2,1)S(1)}, u32[]{:S(2)}, u32[]{:S(2)}) collective-permute-start(bf16[64,2048]{1,0:T(8,128)(2,1)S(1)} %get-tuple-element.49.before.refs_0_), channel_id=1, source_target_pairs={{0,16},{8,24},{16,0},{24,8},{1,17},{9,25},{17,1},{25,9},{2,18},{10... | collective-permute-start | bytes 786440 | tf_op jit(solution)/shard_map/ppermute | solution.py:324
  7.5 14.2 %collective-permute-start.4 = (bf16[32,3072]{1,0:T(8,128)(2,1)}, bf16[32,3072]{1,0:T(8,128)(2,1)S(1)}, u32[]{:S(2)}, u32[]{:S(2)}) collective-permute-start(bf16[32,3072]{1,0:T(8,128)(2,1)} %refs_0_.3), channel_id=1, source_target_pairs={{0,1},{1,0},{2,3},{3,2},{4,5},{5,4},{6,7},{7,6},{8,9},{9,8},{10,11... | collective-permute-start | bytes 589832 | tf_op jit(solution)/shard_map/ppermute | solution.py:324
  9.7 31.0 %collective-permute-start.9 = (bf16[32,3072]{1,0:T(8,128)(2,1)}, bf16[32,3072]{1,0:T(8,128)(2,1)S(1)}, u32[]{:S(2)}, u32[]{:S(2)}) collective-permute-start(bf16[32,3072]{1,0:T(8,128)(2,1)} %refs_0_.3), channel_id=1, source_target_pairs={{0,4},{1,5},{2,6},{3,7},{4,0},{5,1},{6,2},{7,3},{8,12},{9,13},{10,... | collective-permute-start | bytes 589832 | tf_op jit(solution)/shard_map/ppermute | solution.py:324
  12.3 17.6 %collective-permute-start.11 = (bf16[32,3072]{1,0:T(8,128)(2,1)}, bf16[32,3072]{1,0:T(8,128)(2,1)S(1)}, u32[]{:S(2)}, u32[]{:S(2)}) collective-permute-start(bf16[32,3072]{1,0:T(8,128)(2,1)} %refs_0_.3), channel_id=1, source_target_pairs={{0,6},{1,7},{2,4},{3,5},{4,2},{5,3},{6,0},{7,1},{8,14},{9,15},{10,... | collective-permute-start | bytes 589832 | tf_op jit(solution)/shard_map/ppermute | solution.py:324
  13.7 1.0 %copy-start = (bf16[32,3072]{1,0:T(8,128)(2,1)S(1)}, bf16[32,3072]{1,0:T(8,128)(2,1)}, u32[]{:S(2)}) copy-start(bf16[32,3072]{1,0:T(8,128)(2,1)} %refs_0_.3) | copy-start | bytes 589828
  20.0 20.7 %collective-permute-start.1 = (bf16[64,2048]{1,0:T(8,128)(2,1)S(1)}, bf16[64,2048]{1,0:T(8,128)(2,1)S(1)}, u32[]{:S(2)}, u32[]{:S(2)}) collective-permute-start(bf16[64,2048]{1,0:T(8,128)(2,1)S(1)} %next_hidden.3.refs_2_), channel_id=1, source_target_pairs={{0,16},{8,24},{16,0},{24,8},{1,17},{9,25},{17,1},{25,9},{2,18},{10... | collective-permute-start | bytes 786440 | tf_op jit(solution)/shard_map/ppermute | solution.py:324
  21.6 11.6 %collective-permute-start.2 = (bf16[64,2048]{1,0:T(8,128)(2,1)S(1)}, bf16[64,2048]{1,0:T(8,128)(2,1)S(1)}, u32[]{:S(2)}, u32[]{:S(2)}) collective-permute-start(bf16[64,2048]{1,0:T(8,128)(2,1)S(1)} %next_hidden.2.before.refs_1_), channel_id=1, source_target_pairs={{0,16},{8,24},{16,0},{24,8},{1,17},{9,25},{17,1},{25,9},{2,18},{10... | collective-permute-start | bytes 786440 | tf_op jit(solution)/shard_map/ppermute | solution.py:324
  24.3 5.3 %copy-start.1 = (bf16[32,3072]{1,0:T(8,128)(2,1)S(1)}, bf16[32,3072]{1,0:T(8,128)(2,1)}, u32[]{:S(2)}) copy-start(bf16[32,3072]{1,0:T(8,128)(2,1)} %refs_0_.3) | copy-start | bytes 589828
  29.6 13.9 %collective-permute-start.7 = (bf16[32,3072]{1,0:T(8,128)(2,1)S(1)}, bf16[32,3072]{1,0:T(8,128)(2,1)S(1)}, u32[]{:S(2)}, u32[]{:S(2)}) collective-permute-start(bf16[32,3072]{1,0:T(8,128)(2,1)S(1)} %copy-done.1), channel_id=1, source_target_pairs={{0,2},{1,3},{2,0},{3,1},{4,6},{5,7},{6,4},{7,5},{8,10},{9,11},{10,... | collective-permute-start | bytes 589832 | tf_op jit(solution)/shard_map/ppermute | solution.py:324
  29.9 22.0 %collective-permute-start.12 = (bf16[32,3072]{1,0:T(8,128)(2,1)S(1)}, bf16[32,3072]{1,0:T(8,128)(2,1)S(1)}, u32[]{:S(2)}, u32[]{:S(2)}) collective-permute-start(bf16[32,3072]{1,0:T(8,128)(2,1)S(1)} %collective-permute-done.11.refs_6_), channel_id=1, source_target_pairs={{0,1},{1,0},{2,3},{3,2},{4,5},{5,4},{6,7},{7,6},{8,9},{9,8},{10,11... | collective-permute-start | bytes 589832 | tf_op jit(solution)/shard_map/ppermute | solution.py:324
  40.7 11.7 %collective-permute-start.10 = (bf16[32,3072]{1,0:T(8,128)(2,1)S(1)}, bf16[32,3072]{1,0:T(8,128)(2,1)S(1)}, u32[]{:S(2)}, u32[]{:S(2)}) collective-permute-start(bf16[32,3072]{1,0:T(8,128)(2,1)S(1)} %collective-permute-done.9.refs_4_), channel_id=1, source_target_pairs={{0,1},{1,0},{2,3},{3,2},{4,5},{5,4},{6,7},{7,6},{8,9},{9,8},{10,11... | collective-permute-start | bytes 589832 | tf_op jit(solution)/shard_map/ppermute | solution.py:324
  43.5 10.5 %collective-permute-start.8 = (bf16[32,3072]{1,0:T(8,128)(2,1)S(1)}, bf16[32,3072]{1,0:T(8,128)(2,1)S(1)}, u32[]{:S(2)}, u32[]{:S(2)}) collective-permute-start(bf16[32,3072]{1,0:T(8,128)(2,1)S(1)} %collective-permute-done.7.refs_2_), channel_id=1, source_target_pairs={{0,1},{1,0},{2,3},{3,2},{4,5},{5,4},{6,7},{7,6},{8,9},{9,8},{10,11... | collective-permute-start | bytes 589832 | tf_op jit(solution)/shard_map/ppermute | solution.py:324
  49.8 11.5 %collective-permute-start.6 = (bf16[32,3072]{1,0:T(8,128)(2,1)S(1)}, bf16[32,3072]{1,0:T(8,128)(2,1)S(1)}, u32[]{:S(2)}, u32[]{:S(2)}) collective-permute-start(bf16[32,3072]{1,0:T(8,128)(2,1)S(1)} %get-tuple-element.72), channel_id=1, source_target_pairs={{0,1},{1,0},{2,3},{3,2},{4,5},{5,4},{6,7},{7,6},{8,9},{9,8},{10,11... | collective-permute-start | bytes 589832 | tf_op jit(solution)/shard_map/ppermute | solution.py:324
  50.4 27.2 %collective-permute-start.5 = (bf16[32,3072]{1,0:T(8,128)(2,1)S(1)}, bf16[32,3072]{1,0:T(8,128)(2,1)S(1)}, u32[]{:S(2)}, u32[]{:S(2)}) collective-permute-start(bf16[32,3072]{1,0:T(8,128)(2,1)S(1)} %get-tuple-element.70), channel_id=1, source_target_pairs={{0,1},{1,0},{2,3},{3,2},{4,5},{5,4},{6,7},{7,6},{8,9},{9,8},{10,11... | collective-permute-start | bytes 589832 | tf_op jit(solution)/shard_map/ppermute | solution.py:324
  51.9 17.4 %collective-permute-start.14 = (bf16[32,3072]{1,0:T(8,128)(2,1)S(1)}, bf16[32,3072]{1,0:T(8,128)(2,1)S(1)}, u32[]{:S(2)}, u32[]{:S(2)}) collective-permute-start(bf16[32,3072]{1,0:T(8,128)(2,1)S(1)} %get-tuple-element.80), channel_id=1, source_target_pairs={{0,1},{1,0},{2,3},{3,2},{4,5},{5,4},{6,7},{7,6},{8,9},{9,8},{10,11... | collective-permute-start | bytes 589832 | tf_op jit(solution)/shard_map/ppermute | solution.py:324
  52.5 24.5 %collective-permute-start.16 = (bf16[32,3072]{1,0:T(8,128)(2,1)S(1)}, bf16[32,3072]{1,0:T(8,128)(2,1)S(1)}, u32[]{:S(2)}, u32[]{:S(2)}) collective-permute-start(bf16[32,3072]{1,0:T(8,128)(2,1)S(1)} %get-tuple-element.88), channel_id=1, source_target_pairs={{0,1},{1,0},{2,3},{3,2},{4,5},{5,4},{6,7},{7,6},{8,9},{9,8},{10,11... | collective-permute-start | bytes 589832 | tf_op jit(solution)/shard_map/ppermute | solution.py:324
  61.4 16.3 %collective-permute-start.13 = (bf16[32,3072]{1,0:T(8,128)(2,1)S(1)}, bf16[32,3072]{1,0:T(8,128)(2,1)S(1)}, u32[]{:S(2)}, u32[]{:S(2)}) collective-permute-start(bf16[32,3072]{1,0:T(8,128)(2,1)S(1)} %add_convert_fusion.3), channel_id=1, source_target_pairs={{0,4},{1,5},{2,6},{3,7},{4,0},{5,1},{6,2},{7,3},{8,12},{9,13},{10,... | collective-permute-start | bytes 589832 | tf_op jit(solution)/shard_map/ppermute | solution.py:324
  69.4 8.3 %collective-permute-start.15 = (bf16[32,3072]{1,0:T(8,128)(2,1)S(1)}, bf16[32,3072]{1,0:T(8,128)(2,1)S(1)}, u32[]{:S(2)}, u32[]{:S(2)}) collective-permute-start(bf16[32,3072]{1,0:T(8,128)(2,1)S(1)} %add_convert_fusion.2), channel_id=1, source_target_pairs={{0,6},{1,7},{2,4},{3,5},{4,2},{5,3},{6,0},{7,1},{8,14},{9,15},{10,... | collective-permute-start | bytes 589832 | tf_op jit(solution)/shard_map/ppermute | solution.py:324
  77.0 5.7 %collective-permute-start.17 = (bf16[32,3072]{1,0:T(8,128)(2,1)S(1)}, bf16[32,3072]{1,0:T(8,128)(2,1)S(1)}, u32[]{:S(2)}, u32[]{:S(2)}) collective-permute-start(bf16[32,3072]{1,0:T(8,128)(2,1)S(1)} %add_convert_fusion.1), channel_id=1, source_target_pairs={{0,2},{1,3},{2,0},{3,1},{4,6},{5,7},{6,4},{7,5},{8,10},{9,11},{10,... | collective-permute-start | bytes 589832 | tf_op jit(solution)/shard_map/ppermute | solution.py:324

commit v2 on v0

v2 whole, which is shorter than its diff:
```python
import functools

import jax
import jax.numpy as jnp
from jax import lax
from jax.experimental import pallas as pl
from jax.experimental.pallas import tpu as pltpu
from jax.sharding import PartitionSpec as P

COPIES = 6
VMEM = pl.BlockSpec(memory_space=pltpu.VMEM)
HBM = pl.BlockSpec(memory_space=pltpu.HBM)
SMEM = pl.BlockSpec(memory_space=pltpu.SMEM)
CORES = [[0, 1], [2, 3]]


def gelu_slope(value):
    coeff = 0.7978845608028654
    inner = coeff * (value + 0.044715 * value * value * value)
    tanh_val = jnp.tanh(inner)
    return 0.5 * (1.0 + tanh_val) + 0.5 * value * (1.0 - tanh_val * tanh_val) * coeff * (
        1.0 + 3.0 * 0.044715 * value * value
    )


def hidden_grad_of(pre, upstream):
    return (upstream.astype(jnp.float32) * gelu_slope(pre.astype(jnp.float32))).astype(jnp.bfloat16)


def grad_rows(hidden_rows, weight):
    return lax.dot_general(
        hidden_rows, weight, (((1,), (1,)), ((), ())), preferred_element_type=jnp.float32
    )


def outer_sum(input_rows, hidden_rows):
    return lax.dot_general(
        input_rows, hidden_rows, (((0,), (0,)), ((), ())), preferred_element_type=jnp.float32
    )


def general_shards(layer_input, weight, hidden_pre, upstream):
    hidden_grad = hidden_grad_of(hidden_pre, upstream)
    hidden_all = lax.all_gather(hidden_grad, "row", axis=0, tiled=True)
    input_all = lax.all_gather(layer_input, "col", axis=0, tiled=True)
    terms = grad_rows(hidden_all, weight)
    input_sum = lax.psum_scatter(terms, "col", scatter_dimension=0, tiled=True)
    weight_sum = outer_sum(input_all, hidden_all)
    return (input_sum.astype(jnp.bfloat16), weight_sum.astype(jnp.bfloat16))


def slope_columns(pre, up, start, size, outs):
    step = 512

    @pl.loop(0, size // step)
    def _(i):
        here = pl.ds(pl.multiple_of(start + i * step, step), step)
        value = hidden_grad_of(pre[:, here], up[:, here])
        for out, first in outs:
            out[:, pl.ds(pl.multiple_of(first + i * step, step), step)] = value


def hidden_kernel(starts, sizes, pre_hbm, up_hbm, *refs):
    parts, refs = refs[: len(sizes)], refs[len(sizes) :]
    own, pre, up, sems = refs
    copies = []
    for n, (start, size) in enumerate(zip(starts, sizes)):
        cols = pl.ds(start, size)
        for m, (source, target) in enumerate(((pre_hbm, pre), (up_hbm, up))):
            copies.append(pltpu.make_async_copy(source.at[:, cols], target.at[:, cols], sems.at[n, m]))
            copies[-1].start()
    for n, (part, start, size) in enumerate(zip(parts, starts, sizes)):
        copies[2 * n].wait()
        copies[2 * n + 1].wait()
        slope_columns(pre, up, start, size, [(part, 0), (own, start)])


def hidden_parts(pre, up, starts, sizes):
    rows, width = pre.shape
    outs = [(rows, size) for size in sizes] + [(rows, width)]
    return pl.pallas_call(
        functools.partial(hidden_kernel, starts, sizes),
        in_specs=[HBM] * 2,
        out_specs=[VMEM] * len(outs),
        out_shape=[pltpu.VMEM(shape, jnp.bfloat16) for shape in outs],
        scratch_shapes=[
            pltpu.VMEM((rows, width), jnp.bfloat16),
            pltpu.VMEM((rows, width), jnp.bfloat16),
            pltpu.SemaphoreType.DMA((len(sizes), 2)),
        ],
        compiler_params=pltpu.CompilerParams(vmem_limit_bytes=60 << 20),
        cost_estimate=pl.CostEstimate(flops=20 * pre.size, bytes_accessed=6 * pre.size, transcendentals=pre.size),
        name="hidden_grad",
    )(pre, up)


def weight_copies(weight, tiles, sems, start, size):
    rows = weight.shape[0] // COPIES
    return [
        pltpu.make_async_copy(
            weight.at[pl.ds(n * rows, rows), pl.ds(start, size)], tiles.at[pl.ds(n * rows, rows)], sems.at[n]
        )
        for n in range(COPIES)
    ]


def pair_kernel(first, second, out):
    out[0] = first[...]
    out[1] = second[...]


def pair_of(first, second):
    return pl.pallas_call(
        pair_kernel,
        in_specs=[VMEM] * 2,
        out_specs=VMEM,
        out_shape=pltpu.VMEM((2, *first.shape), first.dtype),
        compiler_params=pltpu.CompilerParams(vmem_limit_bytes=16 << 20),
        cost_estimate=pl.CostEstimate(flops=0, bytes_accessed=8 * first.size, transcendentals=0),
        name="pair",
    )(first, second)


def gather_hidden(place_ref, own, sib, far, start, offset, hidden):
    rows, size = own.shape[0], hidden.shape[1]
    cols, here, core = pl.ds(start + offset, size), pl.ds(offset, size), place_ref[3]
    for j, part in enumerate((own.at[:, cols], sib.at[:, cols], far.at[core, :, here], far.at[1 - core, :, here])):
        hidden[pl.ds(rows * j, rows)] = part[...]


def terms_kernel(starts, n, first, last, place_ref, own, sib, far, weight, *refs):
    held, refs = (None, refs) if first else (refs[0], refs[1:])
    if last:
        sends, keeps, refs = refs[:3], refs[3:7], refs[7:]
        total, hidden, tiles, sems = refs
    else:
        total, token, hidden, tiles, sems = refs
        token[...] = jnp.zeros_like(token)
    copies = weight_copies(weight, tiles, sems, starts[n], tiles.shape[1])
    for copy in copies:
        copy.start()
    gather_hidden(place_ref, own, sib, far, starts[n], 0, hidden)
    rows, model = own.shape[0], tiles.shape[0]
    block = model // COPIES
    for i, copy in enumerate(copies):
        copy.wait()
        here = pl.ds(i * block, block)
        term = grad_rows(hidden[...], tiles[here]).reshape(8, rows // 2, block)
        total[:, :, here] = term if first else term + held[:, :, here]

    if last:
        row, z, x = place_ref[0], place_ref[1], place_ref[2]
        slots = [2 * (row ^ z ^ k) for k in range(4)]
        sends[0][0] = total[slots[1] + x].astype(jnp.bfloat16)
        sends[0][1] = total[slots[1] + (1 - x)].astype(jnp.bfloat16)
        for k in (2, 3):
            sends[k - 1][...] = total[slots[k] + (1 - x)].astype(jnp.bfloat16)
            keeps[k][...] = total[slots[k] + x]
        keeps[0][...] = total[slots[0] + x]
        keeps[1][...] = total[slots[0] + (1 - x)]


def terms_part(place, parts, weight, held, starts, sizes, n):
    _, rows, size = parts[2].shape
    model = weight.shape[0]
    first, last = n == 0, n == len(sizes) - 1
    half = rows // 2
    operands = [place, *parts, weight]
    in_specs = [SMEM] + [VMEM] * 3 + [HBM]
    aliases = {}
    if not first:
        if not last:
            aliases[len(operands)] = 0
        operands.append(held)
        in_specs.append(VMEM)
    scratch = [
        pltpu.VMEM((4 * rows, size), jnp.bfloat16),
        pltpu.VMEM((model, size), jnp.bfloat16),
        pltpu.SemaphoreType.DMA((COPIES,)),
    ]
    if last:
        scratch = [pltpu.VMEM((8, half, model), jnp.float32)] + scratch
        out_shape = [pltpu.VMEM((2, half, model), jnp.bfloat16)] + [pltpu.VMEM((half, model), jnp.bfloat16)] * 2
        out_shape += [pltpu.VMEM((half, model), jnp.float32)] * 4
    else:
        out_shape = [pltpu.VMEM((8, half, model), jnp.float32), pltpu.VMEM((8, 128), jnp.float32)]
    return pl.pallas_call(
        functools.partial(terms_kernel, starts, n, first, last),
        in_specs=in_specs,
        out_specs=[VMEM] * len(out_shape),
        out_shape=out_shape,
        scratch_shapes=scratch,
        input_output_aliases=aliases,
        compiler_params=pltpu.CompilerParams(vmem_limit_bytes=40 << 20),
        cost_estimate=pl.CostEstimate(
            flops=8 * rows * size * model, bytes_accessed=2 * size * model, transcendentals=0
        ),
        name="terms",
    )(*operands)


def input_kernel(place_ref, near, next_pair, two, three, crossed, out, held):
    row, z, x = place_ref[0], place_ref[1], place_ref[2]
    half = two.shape[0]
    pairs = (
        (near.at[0], near.at[1]),
        (next_pair.at[0], next_pair.at[1]),
        (two, crossed.at[0]),
        (three, crossed.at[1]),
    )
    for k, (same, other) in enumerate(pairs):
        slot = 2 * (row ^ z ^ k)
        held[slot + x] = same[...]
        held[slot + (1 - x)] = other[...]
    out[...] = held[...].reshape(8 * half, -1).T


def input_columns(place, near, next_pair, two, three, crossed):
    half, model = two.shape
    return pl.pallas_call(
        input_kernel,
        in_specs=[SMEM] + [VMEM] * 5,
        out_specs=VMEM,
        out_shape=pltpu.VMEM((model, 8 * half), jnp.bfloat16),
        scratch_shapes=[pltpu.VMEM((8, half, model), jnp.bfloat16)],
        compiler_params=pltpu.CompilerParams(vmem_limit_bytes=16 << 20),
        cost_estimate=pl.CostEstimate(flops=0, bytes_accessed=32 * half * model, transcendentals=0),
        name="input_columns",
    )(place, near, next_pair, two, three, crossed)


def outer_kernel(start, offset, size, block, first, place_ref, columns_ref, own, sib, far, *refs):
    out, hidden, tiles, sems = refs if first else refs[1:]
    gather_hidden(place_ref, own, sib, far, start, offset, hidden)
    start = start + offset
    slots = tiles.shape[0]
    copies = []
    for n in range(size // block):
        slot = n % slots
        if n >= slots:
            copies[n - slots].wait()
        tiles[slot] = jnp.dot(
            columns_ref[...], hidden[:, pl.ds(n * block, block)], preferred_element_type=jnp.float32
        ).astype(jnp.bfloat16)
        copies.append(
            pltpu.make_async_copy(tiles.at[slot], out.at[:, pl.ds(start + n * block, block)], sems.at[slot])
        )
        copies[-1].start()
    for copy in copies[-slots:]:
        copy.wait()


def outer_part(place, columns, parts, held, start, offset, size, whole):
    model, tokens = columns.shape
    block = 512
    first = held is None
    vmem, hbm = pl.BlockSpec(memory_space=pltpu.VMEM), pl.BlockSpec(memory_space=pl.ANY)
    operands = [place, columns, *parts] + ([] if first else [held])
    slots = min(3, size // block)
    return pl.pallas_call(
        functools.partial(outer_kernel, start, offset, size, block, first),
        in_specs=[pl.BlockSpec(memory_space=pltpu.SMEM)] + [vmem] * 4 + ([] if first else [hbm]),
        out_specs=hbm,
        out_shape=jax.ShapeDtypeStruct((model, whole), jnp.bfloat16),
        scratch_shapes=[
            pltpu.VMEM((tokens, size), jnp.bfloat16),
            pltpu.VMEM((slots, model, block), jnp.bfloat16),
            pltpu.SemaphoreType.DMA((slots,)),
        ],
        input_output_aliases={} if first else {5: 0},
        compiler_params=pltpu.CompilerParams(vmem_limit_bytes=16 << 20),
        cost_estimate=pl.CostEstimate(
            flops=2 * tokens * size * model, bytes_accessed=2 * size * model, transcendentals=0
        ),
        name="outer",
    )(*operands)


def fenced(value, other):
    return lax.optimization_barrier((value, other))[0]


def swap(value, axis, size, bits):
    return lax.ppermute(value, axis, [(n, n ^ bits) for n in range(size)])


def paired_shards(layer_input, weight, hidden_pre, upstream):
    hidden = hidden_pre.shape[1]
    parts = 2
    sizes = [hidden // parts] * parts
    starts = [sum(sizes[:n]) for n in range(parts)]
    row, col = lax.axis_index("row"), lax.axis_index("col")
    place = jnp.stack([row, col // 2, col % 2, row % 2]).astype(jnp.int32)

    across = functools.partial(swap, axis="col", size=8)
    along = functools.partial(swap, axis="row", size=4)

    *sent, own = hidden_parts(hidden_pre, upstream, starts, sizes)
    sib = along(own, bits=1)
    far = [along(part, bits=2) for part in sent]
    crossed_own = across(fenced(layer_input, own), bits=1)
    two = across(fenced(layer_input, own), bits=4)
    near = pair_of(layer_input, fenced(crossed_own, sib))

    far[0] = fenced(far[0], near)
    pairs = [lax.all_gather(far[0], "row", axis=0, axis_index_groups=CORES)]
    three = across(fenced(layer_input, pairs[0]), bits=6)
    next_pair = across(fenced(near, pairs[0]), bits=2)
    held, token = terms_part(place, [own, fenced(sib, two), pairs[0]], weight, None, starts, sizes, 0)
    joint = pair_of(fenced(two, token), three)
    crossed = across(joint, bits=1)
    far[1], joint, held = lax.optimization_barrier((far[1], joint, held))
    pairs.append(lax.all_gather(far[1], "row", axis=0, axis_index_groups=CORES))
    out = terms_part(place, [own, sib, pairs[1]], weight, held, starts, sizes, 1)
    sends, keeps = out[:3], out[3:]

    arrived = across(sends[0], bits=2)
    got = {k: across(sends[k - 1], bits=1) for k in (2, 3)}
    columns = input_columns(place, near, next_pair, two, three, crossed)
    weight_grad, ends = None, {}
    for n, (m, offset, size) in enumerate(((0, 0, 512), (1, 0, 3072), (0, 512, 2560))):
        weight_grad = outer_part(place, columns, [own, sib, pairs[m]], weight_grad, starts[m], offset, size, hidden)
        if n == 0:
            got[2], weight_grad = lax.optimization_barrier((got[2], weight_grad))
            rounded = (keeps[2] + got[2].astype(jnp.float32)).astype(jnp.bfloat16)
            ends[2] = across(rounded, bits=4)
            columns = fenced(columns, rounded)
        if n == 1:
            got[3], arrived, ends[2], weight_grad = lax.optimization_barrier((got[3], arrived, ends[2], weight_grad))
            rounded = (keeps[3] + got[3].astype(jnp.float32)).astype(jnp.bfloat16)
            ends[3] = across(rounded, bits=6)
            turned = (keeps[1] + arrived[1].astype(jnp.float32)).astype(jnp.bfloat16)
            ends[0] = across(turned, bits=1)
            columns = fenced(columns, (rounded, turned))
    input_sum = keeps[0] + arrived[0].astype(jnp.float32)
    for k in (2, 0, 3):
        input_sum = input_sum + ends[k].astype(jnp.float32)
    return (input_sum.astype(jnp.bfloat16), weight_grad)


def solution(mesh):
    in_specs = (P("col", "row"), P("row", "col"), P("row", "col"), P("row", "col"))
    out_specs = (P("col", "row"), P("row", "col"))
    paired = mesh.shape["row"] == 4 and mesh.shape["col"] == 8
    shards = paired_shards if paired else general_shards
    return jax.shard_map(shards, mesh=mesh, in_specs=in_specs, out_specs=out_specs, check_vma=False)
```

time: 175 us -> 76.3 us (0.44)
  waiting for transfers between devices: 69.6 us -> 10.5 us
  local copies, waits for them, and re-layouts: 48.7 us -> 0 us
  Pallas kernels: 0 us -> 40.3 us
  matrix products: 36.3 us -> 0 us
  starting transfers between devices: 0.12 us -> 18.8 us
  between operations: 13.7 us -> 0.78 us
  blocking collectives: 0 us -> 4.91 us
  other arithmetic: 5.04 us -> 0.98 us
    all_gather x2 -> x0, waiting for transfers between devices: 58.1 us -> none  [the longest x1 30.6 us: shards(): lax.all_gather(hidden_grad, 'row', axis=0, tiled=True)]
    unnamed x3 -> x0, local copies, waits for them, and re-layouts: 48.7 us -> none
    pallas_call x0 -> x9, Pallas kernels: none -> 40.3 us  [the longest x3 18.5 us: outer_part(): pl.pallas_call(functools.partial(outer_kernel, start, offset, size, block...]
    dot_general x2 -> x0, matrix products: 36.3 us -> none  [the longest x1 18.8 us: grad_rows(): lax.dot_general(hidden_rows, weight, (((1,), (1,)), ((), ())), preferred_...]
    ppermute x0 -> x14, starting transfers between devices: none -> 18.8 us  [swap(): return lax.ppermute(value, axis, [(n, n ^ bits) for n in range(size)])]
    reduce_scatter x1 -> x0, waiting for transfers between devices: 10.7 us -> none  [shards(): input_sum = lax.psum_scatter(terms, 'col', scatter_dimension=0, tiled=True)]
    ppermute x0 -> x14, waiting for transfers between devices: none -> 10.5 us  [swap(): return lax.ppermute(value, axis, [(n, n ^ bits) for n in range(size)])]
    all_gather x0 -> x2, blocking collectives: none -> 4.91 us  [the longest x1 2.54 us: paired_shards(): pairs.append(lax.all_gather(far[1], 'row', axis=0, axis_index_groups=CORES))]
  transfers between devices with their start and end apart: 3 -> 14, of which waited for: 3 -> 2; matrix products, arithmetic and copies ran while one was open for 49% -> 0% of each run, Pallas kernels for 0% -> 50%
where the time goes in v2:
time: 76.3 us; the launch traced here: 76.2 us
  Pallas kernels  40.3 us (53%)
  starting transfers between devices  18.8 us (25%)
  waiting for transfers between devices  10.5 us (14%)
  blocking collectives  4.91 us (6%)
  other arithmetic  0.98 us (1%)
  between operations  0.78 us (1%)
    ppermute x14, starting transfers between devices, swap(): return lax.ppermute(value, axis, [(n, n ^ bits) for n in range(size)])  18.8 us
    pallas_call x3, Pallas kernels, outer_part(): pl.pallas_call(functools.partial(outer_kernel, start, offset, size, block...  18.5 us
    pallas_call x2, Pallas kernels, terms_part(): pl.pallas_call(functools.partial(terms_kernel, starts, n, first, last), i...  17.3 us
    ppermute x14, waiting for transfers between devices, swap(): return lax.ppermute(value, axis, [(n, n ^ bits) for n in range(size)])  10.5 us
    all_gather x1, blocking collectives, paired_shards(): pairs.append(lax.all_gather(far[1], 'row', axis=0, axis_index_groups=CORES))  2.54 us
    all_gather x1, blocking collectives, paired_shards(): pairs = [lax.all_gather(far[0], 'row', axis=0, axis_index_groups=CORES)]  2.37 us
    pallas_call x1, Pallas kernels, hidden_parts(): pl.pallas_call(functools.partial(hidden_kernel, starts, sizes), in_specs=...  2.36 us
  transfers between devices with their start and end apart: 14, of which 2 were waited for; matrix products, arithmetic and copies ran while one was open for 0% of the time, Pallas kernels for 50%

profile of v2, /device:TPU:0, one launch (start us, length us, event | category | flops | bytes accessed | tf_op | source)
XLA Modules:
  0.0 76.2 jit_solution(6173486356854101444)
XLA Ops:
  0.6 2.4 %hidden_grad.1 = (bf16[64,3072]{1,0:T(8,128)(2,1)S(1)}, bf16[64,3072]{1,0:T(8,128)(2,1)S(1)}, bf16[64,6144]{1,0:T(8,128)(2,1)S(1)}) custom-call(bf16[64,6144]{1,0:T(8,128)(2,1)} %pre_hbm.1, bf16[64,6144]{1,0:T(8,128)(2,1)} %up_hbm.1), custom_call_target="tpu_custom_call" | custom-call | flops 7864320 | bytes 2359296 | tf_op jit(solution)/shard_map/hidden_grad/pallas_call | solution.py:81
  3.0 0.5 collective-permute-start
  3.5 2.6 %collective-permute-start.3 = (bf16[64,3072]{1,0:T(8,128)(2,1)S(1)}, bf16[64,3072]{1,0:T(8,128)(2,1)S(1)}, u32[]{:S(2)}, u32[]{:S(2)}) collective-permute-start(bf16[64,3072]{1,0:T(8,128)(2,1)S(1)} %get-tuple-element.32), channel_id=1, source_target_pairs={{0,16},{8,24},{16,0},{24,8},{1,17},{9,25},{17,1},{25,9},{2,18},{10... | collective-permute-start | bytes 1179656 | tf_op jit(solution)/shard_map/ppermute | solution.py:284
  6.1 2.6 %collective-permute-start.2 = (bf16[32,3072]{1,0:T(8,128)(2,1)}, bf16[32,3072]{1,0:T(8,128)(2,1)S(1)}, u32[]{:S(2)}, u32[]{:S(2)}) collective-permute-start(bf16[32,3072]{1,0:T(8,128)(2,1)} %first.1), channel_id=1, source_target_pairs={{0,4},{1,5},{2,6},{3,7},{4,0},{5,1},{6,2},{7,3},{8,12},{9,13},{10,... | collective-permute-start | bytes 589832 | tf_op jit(solution)/shard_map/ppermute | solution.py:284
  8.7 1.5 %collective-permute-start.4 = (bf16[32,3072]{1,0:T(8,128)(2,1)}, bf16[32,3072]{1,0:T(8,128)(2,1)S(1)}, u32[]{:S(2)}, u32[]{:S(2)}) collective-permute-start(bf16[32,3072]{1,0:T(8,128)(2,1)} %first.1), channel_id=1, source_target_pairs={{0,1},{1,0},{2,3},{3,2},{4,5},{5,4},{6,7},{7,6},{8,9},{9,8},{10,11... | collective-permute-start | bytes 589832 | tf_op jit(solution)/shard_map/ppermute | solution.py:284
  10.8 7.6 %collective-permute-done.2.first.two = bf16[32,3072]{1,0:T(8,128)(2,1)S(1)} collective-permute-done((bf16[32,3072]{1,0:T(8,128)(2,1)}, bf16[32,3072]{1,0:T(8,128)(2,1)S(1)}, u32[]{:S(2)}, u32[]{:S(2)}) %collective-permute-start.2) | collective-permute-done | bytes 196640 | tf_op jit(solution)/shard_map/ppermute | solution.py:284
  18.4 1.0 %pair.2.near = bf16[2,32,3072]{2,1,0:T(8,128)(2,1)S(1)} custom-call(bf16[32,3072]{1,0:T(8,128)(2,1)} %first.1, bf16[32,3072]{1,0:T(8,128)(2,1)S(1)} %collective-permute-done.4.second), custom_call_target="tpu_custom_call" | custom-call | bytes 786432 | tf_op jit(solution)/shard_map/pair/pallas_call | solution.py:113
  19.4 2.4 %all-gather = bf16[128,3072]{1,0:T(8,128)(2,1)S(1)} all-gather(bf16[64,3072]{1,0:T(8,128)(2,1)S(1)} %collective-permute-done.3), channel_id=2, replica_groups={{0,8},{16,24},{1,9},{17,25},{2,10},{18,26},{3,11},{19,27},{4,12},{20,28..., dimensions={0}, use_global_device_ids=true | all-gather | bytes 1179648 | tf_op jit(solution)/shard_map/all_gather | solution.py:306
  21.8 3.5 %collective-permute-start.5 = (bf16[32,3072]{1,0:T(8,128)(2,1)}, bf16[32,3072]{1,0:T(8,128)(2,1)S(1)}, u32[]{:S(2)}, u32[]{:S(2)}) collective-permute-start(bf16[32,3072]{1,0:T(8,128)(2,1)} %first.1), channel_id=1, source_target_pairs={{0,6},{1,7},{2,4},{3,5},{4,2},{5,3},{6,0},{7,1},{8,14},{9,15},{10,... | collective-permute-start | bytes 589832 | tf_op jit(solution)/shard_map/ppermute | solution.py:284
  25.2 8.6 %terms.2 = (f32[8,32,3072]{2,1,0:T(8,128)S(1)}, f32[8,128]{1,0:T(8,128)}) custom-call(s32[4]{0:T(128)S(1)} %pad_add_fusion.place_ref, bf16[64,6144]{1,0:T(8,128)(2,1)S(1)} %get-tuple-element.29.own, bf16[64,6144]{1,0:T(8,128)(2,1)S(1)} %collective-permute-done.sib, bf16[2,64,3072]{2,1,0:T(8,128)(2,1)S(1)} %bitcast.12, bf16[3072,6144]{1,0:T(8,128)(2,1)} %weight.3), custom_call_target="tpu_custom_call" | custom-call | flops 4831838208 | bytes 18874368 | tf_op jit(solution)/shard_map/terms/pallas_call | solution.py:187
  33.9 1.6 %collective-permute-start.10 = (bf16[2,32,3072]{2,1,0:T(8,128)(2,1)S(1)}, bf16[2,32,3072]{2,1,0:T(8,128)(2,1)S(1)}, u32[]{:S(2)}, u32[]{:S(2)}) collective-permute-start(bf16[2,32,3072]{2,1,0:T(8,128)(2,1)S(1)} %pair.3), channel_id=1, source_target_pairs={{0,1},{1,0},{2,3},{3,2},{4,5},{5,4},{6,7},{7,6},{8,9},{9,8},{10,11... | collective-permute-start | bytes 1179656 | tf_op jit(solution)/shard_map/ppermute | solution.py:284
  35.4 2.5 %all-gather.1 = bf16[128,3072]{1,0:T(8,128)(2,1)S(1)} all-gather(bf16[64,3072]{1,0:T(8,128)(2,1)S(1)} %collective-permute-done.1), channel_id=3, replica_groups={{0,8},{16,24},{1,9},{17,25},{2,10},{18,26},{3,11},{19,27},{4,12},{20,28..., dimensions={0}, use_global_device_ids=true | all-gather | bytes 1179648 | tf_op jit(solution)/shard_map/all_gather | solution.py:313
  37.9 8.7 %terms.3 = (bf16[2,32,3072]{2,1,0:T(8,128)(2,1)S(1)}, bf16[32,3072]{1,0:T(8,128)(2,1)S(1)}, bf16[32,3072]{1,0:T(8,128)(2,1)S(1)}, f32[32,3072]{1,0:T(8,128)S(1)}...) custom-call(s32[4]{0:T(128)S(1)} %pad_add_fusion.place_ref, ...), custom_call_target="tpu_custom_call" | custom-call | flops 4831838208 | bytes 18874368 | tf_op jit(solution)/shard_map/terms/pallas_call | solution.py:187
  46.7 0.6 collective-permute-start.8
  47.3 1.5 %collective-permute-start.6 = (bf16[32,3072]{1,0:T(8,128)(2,1)S(1)}, bf16[32,3072]{1,0:T(8,128)(2,1)S(1)}, u32[]{:S(2)}, u32[]{:S(2)}) collective-permute-start(bf16[32,3072]{1,0:T(8,128)(2,1)S(1)} %get-tuple-element.41), channel_id=1, source_target_pairs={{0,1},{1,0},{2,3},{3,2},{4,5},{5,4},{6,7},{7,6},{8,9},{9,8},{10,11... | collective-permute-start | bytes 589832 | tf_op jit(solution)/shard_map/ppermute | solution.py:284
  48.8 2.1 %collective-permute-start.7 = (bf16[2,32,3072]{2,1,0:T(8,128)(2,1)S(1)}, bf16[2,32,3072]{2,1,0:T(8,128)(2,1)S(1)}, u32[]{:S(2)}, u32[]{:S(2)}) collective-permute-start(bf16[2,32,3072]{2,1,0:T(8,128)(2,1)S(1)} %get-tuple-element.42), channel_id=1, source_target_pairs={{0,2},{1,3},{2,0},{3,1},{4,6},{5,7},{6,4},{7,5},{8,10},{9,11},{10,... | collective-permute-start | bytes 1179656 | tf_op jit(solution)/shard_map/ppermute | solution.py:284
  50.8 1.1 %input_columns.1.columns_ref = bf16[3072,256]{1,0:T(8,128)(2,1)S(1)} custom-call(s32[4]{0:T(128)S(1)} %pad_add_fusion.place_ref, bf16[2,32,3072]{2,1,0:T(8,128)(2,1)S(1)} %pair.2.near, bf16[2,32,3072]{2,1,0:T(8,128)(2,1)S(1)} %collective-permute-done.9.next_pair, bf16[32,3072]{1,0:T(8,128)(2,1)S(1)} %collective-permute-done.2.first.two, ...), custom_call_target="tpu_custom_call" | custom-call | bytes 3145728 | tf_op jit(solution)/shard_map/input_columns/pallas_call | solution.py:220
  51.9 3.2 %outer.3.refs_0_ = bf16[3072,6144]{1,0:T(8,128)(2,1)} custom-call(s32[4]{0:T(128)S(1)} %pad_add_fusion.place_ref, bf16[3072,256]{1,0:T(8,128)(2,1)S(1)} %input_columns.1.columns_ref, bf16[64,6144]{1,0:T(8,128)(2,1)S(1)} %get-tuple-element.29.own, bf16[64,6144]{1,0:T(8,128)(2,1)S(1)} %collective-permute-done.sib, bf16[2,64,3072]{2,1,0:T(8,128)(2,1)S(1)} %bitcast.13), custom_call_target="tpu_custom_call" | custom-call | flops 805306368 | bytes 3145728 | tf_op jit(solution)/shard_map/outer/pallas_call | solution.py:260
  55.5 8.2 %outer.4.refs_0_ = bf16[3072,6144]{1,0:T(8,128)(2,1)} custom-call(s32[4]{0:T(128)S(1)} %pad_add_fusion.place_ref, bf16[3072,256]{1,0:T(8,128)(2,1)S(1)} %input_columns.1.columns_ref, bf16[64,6144]{1,0:T(8,128)(2,1)S(1)} %get-tuple-element.29.own, bf16[64,6144]{1,0:T(8,128)(2,1)S(1)} %collective-permute-done.sib, ...), custom_call_target="tpu_custom_call", output_to_operand_aliasing={{}: (5, {})} | custom-call | flops 4831838208 | bytes 18874368 | tf_op jit(solution)/shard_map/outer/pallas_call | solution.py:260
  63.7 2.8 %collective-permute-done.11 = bf16[32,3072]{1,0:T(8,128)(2,1)S(1)} collective-permute-done((bf16[32,3072]{1,0:T(8,128)(2,1)S(1)}, bf16[32,3072]{1,0:T(8,128)(2,1)S(1)}, u32[]{:S(2)}, u32[]{:S(2)}) %collective-permute-start.11) | collective-permute-done | bytes 196640 | tf_op jit(solution)/shard_map/ppermute | solution.py:284
  66.5 0.8 %collective-permute-start.13 = (bf16[32,3072]{1,0:T(8,128)(2,1)S(1)}, bf16[32,3072]{1,0:T(8,128)(2,1)S(1)}, u32[]{:S(2)}, u32[]{:S(2)}) collective-permute-start(bf16[32,3072]{1,0:T(8,128)(2,1)S(1)} %add_convert_fusion), channel_id=1, source_target_pairs={{0,6},{1,7},{2,4},{3,5},{4,2},{5,3},{6,0},{7,1},{8,14},{9,15},{10,... | collective-permute-start | bytes 589832 | tf_op jit(solution)/shard_map/ppermute | solution.py:284
  67.4 0.8 %collective-permute-start.12 = (bf16[32,3072]{1,0:T(8,128)(2,1)S(1)}, bf16[32,3072]{1,0:T(8,128)(2,1)S(1)}, u32[]{:S(2)}, u32[]{:S(2)}) collective-permute-start(bf16[32,3072]{1,0:T(8,128)(2,1)S(1)} %fusion), channel_id=1, source_target_pairs={{0,1},{1,0},{2,3},{3,2},{4,5},{5,4},{6,7},{7,6},{8,9},{9,8},{10,11... | collective-permute-start | bytes 589832 | tf_op jit(solution)/shard_map/ppermute | solution.py:284
  68.1 7.2 %outer.5 = bf16[3072,6144]{1,0:T(8,128)(2,1)} custom-call(s32[4]{0:T(128)S(1)} %pad_add_fusion.place_ref, bf16[3072,256]{1,0:T(8,128)(2,1)S(1)} %input_columns.1.columns_ref, bf16[64,6144]{1,0:T(8,128)(2,1)S(1)} %get-tuple-element.29.own, bf16[64,6144]{1,0:T(8,128)(2,1)S(1)} %collective-permute-done.sib, ...), custom_call_target="tpu_custom_call", output_to_operand_aliasing={{}: (5, {})} | custom-call | flops 4026531840 | bytes 15728640 | tf_op jit(solution)/shard_map/outer/pallas_call | solution.py:260
  75.4 0.8 %fusion.4 = bf16[32,3072]{1,0:T(8,128)(2,1)} fusion(f32[32,3072]{1,0:T(8,128)S(1)} %get-tuple-element.40, bf16[32,3072]{1,0:T(8,128)(2,1)S(1)} %collective-permute-done.13, bf16[32,3072]{1,0:T(8,128)(2,1)S(1)} %collective-permute-done.12, bf16[32,3072]{1,0:T(8,128)(2,1)S(1)} %collective-permute-done.11, bf16[2,32,3072]{2,1,0:T(8,128)(2,1)S(1)} %collective-permute-done.7), kind=kLoop, calls=%fused_computation.6 | loop fusion | flops 884736 | bytes 1376256 | tf_op jit(solution)/shard_map/convert_element_type | solution.py:338
  (20 shorter events, 1.1 us)
Async XLA Ops:
  3.0 15.4 %collective-permute-start = (bf16[64,6144]{1,0:T(8,128)(2,1)S(1)}, bf16[64,6144]{1,0:T(8,128)(2,1)S(1)}, u32[]{:S(2)}, u32[]{:S(2)}) collective-permute-start(bf16[64,6144]{1,0:T(8,128)(2,1)S(1)} %get-tuple-element.29.own), channel_id=1, source_target_pairs={{0,8},{8,0},{16,24},{24,16},{1,9},{9,1},{17,25},{25,17},{2,10},{10... | collective-permute-start | bytes 2359304 | tf_op jit(solution)/shard_map/ppermute | solution.py:284
  3.5 15.9 %collective-permute-start.3 = (bf16[64,3072]{1,0:T(8,128)(2,1)S(1)}, bf16[64,3072]{1,0:T(8,128)(2,1)S(1)}, u32[]{:S(2)}, u32[]{:S(2)}) collective-permute-start(bf16[64,3072]{1,0:T(8,128)(2,1)S(1)} %get-tuple-element.32), channel_id=1, source_target_pairs={{0,16},{8,24},{16,0},{24,8},{1,17},{9,25},{17,1},{25,9},{2,18},{10... | collective-permute-start | bytes 1179656 | tf_op jit(solution)/shard_map/ppermute | solution.py:284
  6.1 12.3 %collective-permute-start.2 = (bf16[32,3072]{1,0:T(8,128)(2,1)}, bf16[32,3072]{1,0:T(8,128)(2,1)S(1)}, u32[]{:S(2)}, u32[]{:S(2)}) collective-permute-start(bf16[32,3072]{1,0:T(8,128)(2,1)} %first.1), channel_id=1, source_target_pairs={{0,4},{1,5},{2,6},{3,7},{4,0},{5,1},{6,2},{7,3},{8,12},{9,13},{10,... | collective-permute-start | bytes 589832 | tf_op jit(solution)/shard_map/ppermute | solution.py:284
  8.7 9.7 %collective-permute-start.4 = (bf16[32,3072]{1,0:T(8,128)(2,1)}, bf16[32,3072]{1,0:T(8,128)(2,1)S(1)}, u32[]{:S(2)}, u32[]{:S(2)}) collective-permute-start(bf16[32,3072]{1,0:T(8,128)(2,1)} %first.1), channel_id=1, source_target_pairs={{0,1},{1,0},{2,3},{3,2},{4,5},{5,4},{6,7},{7,6},{8,9},{9,8},{10,11... | collective-permute-start | bytes 589832 | tf_op jit(solution)/shard_map/ppermute | solution.py:284
  10.2 25.2 %collective-permute-start.1 = (bf16[64,3072]{1,0:T(8,128)(2,1)S(1)}, bf16[64,3072]{1,0:T(8,128)(2,1)S(1)}, u32[]{:S(2)}, u32[]{:S(2)}) collective-permute-start(bf16[64,3072]{1,0:T(8,128)(2,1)S(1)} %get-tuple-element.30), channel_id=1, source_target_pairs={{0,16},{8,24},{16,0},{24,8},{1,17},{9,25},{17,1},{25,9},{2,18},{10... | collective-permute-start | bytes 1179656 | tf_op jit(solution)/shard_map/ppermute | solution.py:284
  21.8 12.1 %collective-permute-start.5 = (bf16[32,3072]{1,0:T(8,128)(2,1)}, bf16[32,3072]{1,0:T(8,128)(2,1)S(1)}, u32[]{:S(2)}, u32[]{:S(2)}) collective-permute-start(bf16[32,3072]{1,0:T(8,128)(2,1)} %first.1), channel_id=1, source_target_pairs={{0,6},{1,7},{2,4},{3,5},{4,2},{5,3},{6,0},{7,1},{8,14},{9,15},{10,... | collective-permute-start | bytes 589832 | tf_op jit(solution)/shard_map/ppermute | solution.py:284
  25.2 25.6 %collective-permute-start.9 = (bf16[2,32,3072]{2,1,0:T(8,128)(2,1)S(1)}, bf16[2,32,3072]{2,1,0:T(8,128)(2,1)S(1)}, u32[]{:S(2)}, u32[]{:S(2)}) collective-permute-start(bf16[2,32,3072]{2,1,0:T(8,128)(2,1)S(1)} %pair.2.near), channel_id=1, source_target_pairs={{0,2},{1,3},{2,0},{3,1},{4,6},{5,7},{6,4},{7,5},{8,10},{9,11},{10,... | collective-permute-start | bytes 1179656 | tf_op jit(solution)/shard_map/ppermute | solution.py:284
  33.9 17.0 %collective-permute-start.10 = (bf16[2,32,3072]{2,1,0:T(8,128)(2,1)S(1)}, bf16[2,32,3072]{2,1,0:T(8,128)(2,1)S(1)}, u32[]{:S(2)}, u32[]{:S(2)}) collective-permute-start(bf16[2,32,3072]{2,1,0:T(8,128)(2,1)S(1)} %pair.3), channel_id=1, source_target_pairs={{0,1},{1,0},{2,3},{3,2},{4,5},{5,4},{6,7},{7,6},{8,9},{9,8},{10,11... | collective-permute-start | bytes 1179656 | tf_op jit(solution)/shard_map/ppermute | solution.py:284
  46.7 8.5 %collective-permute-start.8 = (bf16[32,3072]{1,0:T(8,128)(2,1)S(1)}, bf16[32,3072]{1,0:T(8,128)(2,1)S(1)}, u32[]{:S(2)}, u32[]{:S(2)}) collective-permute-start(bf16[32,3072]{1,0:T(8,128)(2,1)S(1)} %get-tuple-element.44), channel_id=1, source_target_pairs={{0,1},{1,0},{2,3},{3,2},{4,5},{5,4},{6,7},{7,6},{8,9},{9,8},{10,11... | collective-permute-start | bytes 589832 | tf_op jit(solution)/shard_map/ppermute | solution.py:284
  47.3 16.4 %collective-permute-start.6 = (bf16[32,3072]{1,0:T(8,128)(2,1)S(1)}, bf16[32,3072]{1,0:T(8,128)(2,1)S(1)}, u32[]{:S(2)}, u32[]{:S(2)}) collective-permute-start(bf16[32,3072]{1,0:T(8,128)(2,1)S(1)} %get-tuple-element.41), channel_id=1, source_target_pairs={{0,1},{1,0},{2,3},{3,2},{4,5},{5,4},{6,7},{7,6},{8,9},{9,8},{10,11... | collective-permute-start | bytes 589832 | tf_op jit(solution)/shard_map/ppermute | solution.py:284
  48.8 14.9 %collective-permute-start.7 = (bf16[2,32,3072]{2,1,0:T(8,128)(2,1)S(1)}, bf16[2,32,3072]{2,1,0:T(8,128)(2,1)S(1)}, u32[]{:S(2)}, u32[]{:S(2)}) collective-permute-start(bf16[2,32,3072]{2,1,0:T(8,128)(2,1)S(1)} %get-tuple-element.42), channel_id=1, source_target_pairs={{0,2},{1,3},{2,0},{3,1},{4,6},{5,7},{6,4},{7,5},{8,10},{9,11},{10,... | collective-permute-start | bytes 1179656 | tf_op jit(solution)/shard_map/ppermute | solution.py:284
  55.2 11.3 %collective-permute-start.11 = (bf16[32,3072]{1,0:T(8,128)(2,1)S(1)}, bf16[32,3072]{1,0:T(8,128)(2,1)S(1)}, u32[]{:S(2)}, u32[]{:S(2)}) collective-permute-start(bf16[32,3072]{1,0:T(8,128)(2,1)S(1)} %add_convert_fusion.1), channel_id=1, source_target_pairs={{0,4},{1,5},{2,6},{3,7},{4,0},{5,1},{6,2},{7,3},{8,12},{9,13},{10,... | collective-permute-start | bytes 589832 | tf_op jit(solution)/shard_map/ppermute | solution.py:284
  66.5 8.8 %collective-permute-start.13 = (bf16[32,3072]{1,0:T(8,128)(2,1)S(1)}, bf16[32,3072]{1,0:T(8,128)(2,1)S(1)}, u32[]{:S(2)}, u32[]{:S(2)}) collective-permute-start(bf16[32,3072]{1,0:T(8,128)(2,1)S(1)} %add_convert_fusion), channel_id=1, source_target_pairs={{0,6},{1,7},{2,4},{3,5},{4,2},{5,3},{6,0},{7,1},{8,14},{9,15},{10,... | collective-permute-start | bytes 589832 | tf_op jit(solution)/shard_map/ppermute | solution.py:284
  67.4 8.0 %collective-permute-start.12 = (bf16[32,3072]{1,0:T(8,128)(2,1)S(1)}, bf16[32,3072]{1,0:T(8,128)(2,1)S(1)}, u32[]{:S(2)}, u32[]{:S(2)}) collective-permute-start(bf16[32,3072]{1,0:T(8,128)(2,1)S(1)} %fusion), channel_id=1, source_target_pairs={{0,1},{1,0},{2,3},{3,2},{4,5},{5,4},{6,7},{7,6},{8,9},{9,8},{10,11... | collective-permute-start | bytes 589832 | tf_op jit(solution)/shard_map/ppermute | solution.py:284

commit v3 on v2

--- a/solution.py
+++ b/solution.py
@@ -11,7 +11,6 @@
 VMEM = pl.BlockSpec(memory_space=pltpu.VMEM)
 HBM = pl.BlockSpec(memory_space=pltpu.HBM)
 SMEM = pl.BlockSpec(memory_space=pltpu.SMEM)
-CORES = [[0, 1], [2, 3]]
 
 
 def gelu_slope(value):
@@ -121,25 +120,24 @@
     )(first, second)
 
 
-def gather_hidden(place_ref, own, sib, far, start, offset, hidden):
-    rows, size = own.shape[0], hidden.shape[1]
-    cols, here, core = pl.ds(start + offset, size), pl.ds(offset, size), place_ref[3]
-    for j, part in enumerate((own.at[:, cols], sib.at[:, cols], far.at[core, :, here], far.at[1 - core, :, here])):
+def gather_hidden(own, sib, far, farsib, start, offset, hidden):
+    rows, size = far.shape[0], hidden.shape[1]
+    cols, here = pl.ds(start + offset, size), pl.ds(offset, size)
+    for j, part in enumerate((own.at[:, cols], sib.at[:, cols], far.at[:, here], farsib.at[:, here])):
         hidden[pl.ds(rows * j, rows)] = part[...]
 
 
-def terms_kernel(starts, n, first, last, place_ref, own, sib, far, weight, *refs):
+def terms_kernel(starts, n, first, last, place_ref, own, sib, far, farsib, weight, *refs):
     held, refs = (None, refs) if first else (refs[0], refs[1:])
     if last:
         sends, keeps, refs = refs[:3], refs[3:7], refs[7:]
         total, hidden, tiles, sems = refs
     else:
-        total, token, hidden, tiles, sems = refs
-        token[...] = jnp.zeros_like(token)
+        total, hidden, tiles, sems = refs
     copies = weight_copies(weight, tiles, sems, starts[n], tiles.shape[1])
     for copy in copies:
         copy.start()
-    gather_hidden(place_ref, own, sib, far, starts[n], 0, hidden)
+    gather_hidden(own, sib, far, farsib, starts[n], 0, hidden)
     rows, model = own.shape[0], tiles.shape[0]
     block = model // COPIES
     for i, copy in enumerate(copies):
@@ -161,12 +159,12 @@
 
 
 def terms_part(place, parts, weight, held, starts, sizes, n):
-    _, rows, size = parts[2].shape
+    rows, size = parts[2].shape
     model = weight.shape[0]
     first, last = n == 0, n == len(sizes) - 1
     half = rows // 2
     operands = [place, *parts, weight]
-    in_specs = [SMEM] + [VMEM] * 3 + [HBM]
+    in_specs = [SMEM] + [VMEM] * 4 + [HBM]
     aliases = {}
     if not first:
         if not last:
@@ -183,7 +181,7 @@
         out_shape = [pltpu.VMEM((2, half, model), jnp.bfloat16)] + [pltpu.VMEM((half, model), jnp.bfloat16)] * 2
         out_shape += [pltpu.VMEM((half, model), jnp.float32)] * 4
     else:
-        out_shape = [pltpu.VMEM((8, half, model), jnp.float32), pltpu.VMEM((8, 128), jnp.float32)]
+        out_shape = [pltpu.VMEM((8, half, model), jnp.float32)]
     return pl.pallas_call(
         functools.partial(terms_kernel, starts, n, first, last),
         in_specs=in_specs,
@@ -229,9 +227,9 @@
     )(place, near, next_pair, two, three, crossed)
 
 
-def outer_kernel(start, offset, size, block, first, place_ref, columns_ref, own, sib, far, *refs):
+def outer_kernel(start, offset, size, block, first, columns_ref, own, sib, far, farsib, *refs):
     out, hidden, tiles, sems = refs if first else refs[1:]
-    gather_hidden(place_ref, own, sib, far, start, offset, hidden)
+    gather_hidden(own, sib, far, farsib, start, offset, hidden)
     start = start + offset
     slots = tiles.shape[0]
     copies = []
@@ -250,16 +248,16 @@
         copy.wait()
 
 
-def outer_part(place, columns, parts, held, start, offset, size, whole):
+def outer_part(columns, parts, held, start, offset, size, whole):
     model, tokens = columns.shape
     block = 512
     first = held is None
-    vmem, hbm = pl.BlockSpec(memory_space=pltpu.VMEM), pl.BlockSpec(memory_space=pl.ANY)
-    operands = [place, columns, *parts] + ([] if first else [held])
+    hbm = pl.BlockSpec(memory_space=pl.ANY)
+    operands = [columns, *parts] + ([] if first else [held])
     slots = min(3, size // block)
     return pl.pallas_call(
         functools.partial(outer_kernel, start, offset, size, block, first),
-        in_specs=[pl.BlockSpec(memory_space=pltpu.SMEM)] + [vmem] * 4 + ([] if first else [hbm]),
+        in_specs=[VMEM] * 5 + ([] if first else [hbm]),
         out_specs=hbm,
         out_shape=jax.ShapeDtypeStruct((model, whole), jnp.bfloat16),
         scratch_shapes=[
@@ -276,8 +274,8 @@
     )(*operands)
 
 
-def fenced(value, other):
-    return lax.optimization_barrier((value, other))[0]
+def tied(*values):
+    return lax.optimization_barrier(values)
 
 
 def swap(value, axis, size, bits):
@@ -286,11 +284,10 @@
 
 def paired_shards(layer_input, weight, hidden_pre, upstream):
     hidden = hidden_pre.shape[1]
-    parts = 2
-    sizes = [hidden // parts] * parts
-    starts = [sum(sizes[:n]) for n in range(parts)]
+    sizes = [hidden // 2] * 2
+    starts = [0, hidden // 2]
     row, col = lax.axis_index("row"), lax.axis_index("col")
-    place = jnp.stack([row, col // 2, col % 2, row % 2]).astype(jnp.int32)
+    place = jnp.stack([row, col // 2, col % 2]).astype(jnp.int32)
 
     across = functools.partial(swap, axis="col", size=8)
     along = functools.partial(swap, axis="row", size=4)
@@ -298,43 +295,43 @@
     *sent, own = hidden_parts(hidden_pre, upstream, starts, sizes)
     sib = along(own, bits=1)
     far = [along(part, bits=2) for part in sent]
-    crossed_own = across(fenced(layer_input, own), bits=1)
-    two = across(fenced(layer_input, own), bits=4)
-    near = pair_of(layer_input, fenced(crossed_own, sib))
-
-    far[0] = fenced(far[0], near)
-    pairs = [lax.all_gather(far[0], "row", axis=0, axis_index_groups=CORES)]
-    three = across(fenced(layer_input, pairs[0]), bits=6)
-    next_pair = across(fenced(near, pairs[0]), bits=2)
-    held, token = terms_part(place, [own, fenced(sib, two), pairs[0]], weight, None, starts, sizes, 0)
-    joint = pair_of(fenced(two, token), three)
+    crossed_own, two = across(layer_input, bits=1), across(layer_input, bits=4)
+    near = pair_of(layer_input, crossed_own)
+
+    far[0], near, two = tied(far[0], near, two)
+    source, far[0] = tied(layer_input, far[0])
+    parts = [[own, sib, far[0], along(far[0], bits=1)]]
+    three, next_pair = across(source, bits=6), across(near, bits=2)
+    held, = terms_part(place, parts[0], weight, None, starts, sizes, 0)
+    two, held = tied(two, held)
+    joint, far[1] = tied(pair_of(two, three), far[1])
     crossed = across(joint, bits=1)
-    far[1], joint, held = lax.optimization_barrier((far[1], joint, held))
-    pairs.append(lax.all_gather(far[1], "row", axis=0, axis_index_groups=CORES))
-    out = terms_part(place, [own, sib, pairs[1]], weight, held, starts, sizes, 1)
+    parts.append([own, sib, far[1], along(far[1], bits=1)])
+    out = terms_part(place, parts[1], weight, held, starts, sizes, 1)
     sends, keeps = out[:3], out[3:]
 
     arrived = across(sends[0], bits=2)
-    got = {k: across(sends[k - 1], bits=1) for k in (2, 3)}
+    got = [across(sends[1], bits=1)]
     columns = input_columns(place, near, next_pair, two, three, crossed)
-    weight_grad, ends = None, {}
-    for n, (m, offset, size) in enumerate(((0, 0, 512), (1, 0, 3072), (0, 512, 2560))):
-        weight_grad = outer_part(place, columns, [own, sib, pairs[m]], weight_grad, starts[m], offset, size, hidden)
-        if n == 0:
-            got[2], weight_grad = lax.optimization_barrier((got[2], weight_grad))
-            rounded = (keeps[2] + got[2].astype(jnp.float32)).astype(jnp.bfloat16)
-            ends[2] = across(rounded, bits=4)
-            columns = fenced(columns, rounded)
-        if n == 1:
-            got[3], arrived, ends[2], weight_grad = lax.optimization_barrier((got[3], arrived, ends[2], weight_grad))
-            rounded = (keeps[3] + got[3].astype(jnp.float32)).astype(jnp.bfloat16)
-            ends[3] = across(rounded, bits=6)
-            turned = (keeps[1] + arrived[1].astype(jnp.float32)).astype(jnp.bfloat16)
-            ends[0] = across(turned, bits=1)
-            columns = fenced(columns, (rounded, turned))
+    small = 512
+    weight_grad = outer_part(columns, parts[0], None, starts[0], 0, small, hidden)
+    got[0], weight_grad = tied(got[0], weight_grad)
+    rounded = (keeps[2] + got[0].astype(jnp.float32)).astype(jnp.bfloat16)
+    rounded, weight_grad, late = tied(rounded, weight_grad, sends[2])
+    ends = [across(rounded, bits=4)]
+    got.append(across(late, bits=1))
+    weight_grad = outer_part(columns, parts[1], weight_grad, starts[1], 0, sizes[1], hidden)
+
+    got[1], arrived, ends[0], weight_grad = tied(got[1], arrived, ends[0], weight_grad)
+    rounded = (keeps[3] + got[1].astype(jnp.float32)).astype(jnp.bfloat16)
+    turned = (keeps[1] + arrived[1].astype(jnp.float32)).astype(jnp.bfloat16)
+    rounded, turned, weight_grad = tied(rounded, turned, weight_grad)
+    ends += [across(rounded, bits=6), across(turned, bits=1)]
+    weight_grad = outer_part(columns, parts[0], weight_grad, starts[0], small, sizes[0] - small, hidden)
+
     input_sum = keeps[0] + arrived[0].astype(jnp.float32)
-    for k in (2, 0, 3):
-        input_sum = input_sum + ends[k].astype(jnp.float32)
+    for n in (0, 2, 1):
+        input_sum = input_sum + ends[n].astype(jnp.float32)
     return (input_sum.astype(jnp.bfloat16), weight_grad)
 
 

time: 76.3 us -> 74.2 us (0.972)
  blocking collectives: 4.91 us -> 0 us
  starting transfers between devices: 18.8 us -> 21.6 us
  Pallas kernels: 40.3 us -> 38.5 us
  local copies, waits for them, and re-layouts: 0 us -> 0.93 us
  waiting for transfers between devices: 10.5 us -> 11.4 us
    all_gather x2 -> x0, blocking collectives: 4.91 us -> none  [the longest x1 2.54 us: paired_shards(): pairs.append(lax.all_gather(far[1], 'row', axis=0, axis_index_groups=CORES))]
    ppermute x14 -> x16, starting transfers between devices: 18.8 us -> 21.6 us  [swap(): return lax.ppermute(value, axis, [(n, n ^ bits) for n in range(size)])]
    pallas_call x3, Pallas kernels: 18.5 us -> 16.9 us  [outer_part(): pl.pallas_call(functools.partial(outer_kernel, start, offset, size, block...]
    pallas_call x2, Pallas kernels: 0.98 us -> 0.05 us  [pair_of(): pl.pallas_call(pair_kernel, in_specs=[VMEM] * 2, out_specs=VMEM, out_shap...]
    unnamed x0 -> x2, local copies, waits for them, and re-layouts: none -> 0.93 us
    ppermute x14 -> x16, waiting for transfers between devices: 10.5 us -> 11.4 us  [swap(): return lax.ppermute(value, axis, [(n, n ^ bits) for n in range(size)])]
  transfers between devices with their start and end apart: 14 -> 16, of which waited for: 2 -> 5; matrix products, arithmetic and copies ran while one was open for 0% -> 0% of each run, Pallas kernels for 50% -> 48%
where the time goes in v3:
time: 74.2 us; the launch traced here: 74 us
  Pallas kernels  38.5 us (52%)
  starting transfers between devices  21.6 us (29%)
  waiting for transfers between devices  11.4 us (15%)
  other arithmetic  0.97 us (1%)
  local copies, waits for them, and re-layouts  0.93 us (1%)
  between operations  0.77 us (1%)
    ppermute x16, starting transfers between devices, swap(): return lax.ppermute(value, axis, [(n, n ^ bits) for n in range(size)])  21.6 us
    pallas_call x2, Pallas kernels, terms_part(): pl.pallas_call(functools.partial(terms_kernel, starts, n, first, last), i...  17.3 us
    pallas_call x3, Pallas kernels, outer_part(): pl.pallas_call(functools.partial(outer_kernel, start, offset, size, block...  16.9 us
    ppermute x16, waiting for transfers between devices, swap(): return lax.ppermute(value, axis, [(n, n ^ bits) for n in range(size)])  11.4 us
    pallas_call x1, Pallas kernels, hidden_parts(): pl.pallas_call(functools.partial(hidden_kernel, starts, sizes), in_specs=...  3.11 us
  transfers between devices with their start and end apart: 16, of which 5 were waited for; matrix products, arithmetic and copies ran while one was open for 0% of the time, Pallas kernels for 48%

profile of v3, /device:TPU:0, one launch (start us, length us, event | category | flops | bytes accessed | tf_op | source)
XLA Modules:
  0.0 74.0 jit_solution(14929655310760646699)
XLA Ops:
  0.6 3.1 %hidden_grad.1 = (bf16[64,3072]{1,0:T(8,128)(2,1)S(1)}, bf16[64,3072]{1,0:T(8,128)(2,1)}, bf16[64,6144]{1,0:T(8,128)(2,1)S(1)}) custom-call(bf16[64,6144]{1,0:T(8,128)(2,1)} %pre_hbm.1, bf16[64,6144]{1,0:T(8,128)(2,1)} %up_hbm.1), custom_call_target="tpu_custom_call" | custom-call | flops 7864320 | bytes 2359296 | tf_op jit(solution)/shard_map/hidden_grad/pallas_call | solution.py:80
  3.7 3.0 %collective-permute-start.1 = (bf16[64,3072]{1,0:T(8,128)(2,1)S(1)}, bf16[64,3072]{1,0:T(8,128)(2,1)S(1)}, u32[]{:S(2)}, u32[]{:S(2)}) collective-permute-start(bf16[64,3072]{1,0:T(8,128)(2,1)S(1)} %get-tuple-element.34), channel_id=1, source_target_pairs={{0,16},{8,24},{16,0},{24,8},{1,17},{9,25},{17,1},{25,9},{2,18},{10... | collective-permute-start | bytes 1179656 | tf_op jit(solution)/shard_map/ppermute | solution.py:282
  6.8 1.5 %collective-permute-start.2 = (bf16[32,3072]{1,0:T(8,128)(2,1)}, bf16[32,3072]{1,0:T(8,128)(2,1)S(1)}, u32[]{:S(2)}, u32[]{:S(2)}) collective-permute-start(bf16[32,3072]{1,0:T(8,128)(2,1)} %first.1), channel_id=1, source_target_pairs={{0,1},{1,0},{2,3},{3,2},{4,5},{5,4},{6,7},{7,6},{8,9},{9,8},{10,11... | collective-permute-start | bytes 589832 | tf_op jit(solution)/shard_map/ppermute | solution.py:282
  8.3 2.6 %collective-permute-start.3 = (bf16[32,3072]{1,0:T(8,128)(2,1)}, bf16[32,3072]{1,0:T(8,128)(2,1)S(1)}, u32[]{:S(2)}, u32[]{:S(2)}) collective-permute-start(bf16[32,3072]{1,0:T(8,128)(2,1)} %first.1), channel_id=1, source_target_pairs={{0,4},{1,5},{2,6},{3,7},{4,0},{5,1},{6,2},{7,3},{8,12},{9,13},{10,... | collective-permute-start | bytes 589832 | tf_op jit(solution)/shard_map/ppermute | solution.py:282
  10.9 3.4 %collective-permute-done.2.second = bf16[32,3072]{1,0:T(8,128)(2,1)S(1)} collective-permute-done((bf16[32,3072]{1,0:T(8,128)(2,1)}, bf16[32,3072]{1,0:T(8,128)(2,1)S(1)}, u32[]{:S(2)}, u32[]{:S(2)}) %collective-permute-start.2) | collective-permute-done | bytes 196640 | tf_op jit(solution)/shard_map/ppermute | solution.py:282
  14.3 0.9 %copy-done = bf16[32,3072]{1,0:T(8,128)(2,1)S(1)} copy-done((bf16[32,3072]{1,0:T(8,128)(2,1)S(1)}, bf16[32,3072]{1,0:T(8,128)(2,1)}, u32[]{:S(2)}) %copy-start) | copy-done | bytes 196632
  15.3 5.4 %collective-permute-done.3.first.two = bf16[32,3072]{1,0:T(8,128)(2,1)S(1)} collective-permute-done((bf16[32,3072]{1,0:T(8,128)(2,1)}, bf16[32,3072]{1,0:T(8,128)(2,1)S(1)}, u32[]{:S(2)}, u32[]{:S(2)}) %collective-permute-start.3) | collective-permute-done | bytes 196640 | tf_op jit(solution)/shard_map/ppermute | solution.py:282
  21.2 3.5 %collective-permute-start.5 = (bf16[32,3072]{1,0:T(8,128)(2,1)}, bf16[32,3072]{1,0:T(8,128)(2,1)S(1)}, u32[]{:S(2)}, u32[]{:S(2)}) collective-permute-start(bf16[32,3072]{1,0:T(8,128)(2,1)} %first.1), channel_id=1, source_target_pairs={{0,6},{1,7},{2,4},{3,5},{4,2},{5,3},{6,0},{7,1},{8,14},{9,15},{10,... | collective-permute-start | bytes 589832 | tf_op jit(solution)/shard_map/ppermute | solution.py:282
  24.8 8.5 %terms.2.refs_0_ = f32[8,32,3072]{2,1,0:T(8,128)S(1)} custom-call(s32[3]{0:T(128)S(1)} %pad_add_fusion.place_ref, bf16[64,6144]{1,0:T(8,128)(2,1)S(1)} %get-tuple-element.33.own, bf16[64,6144]{1,0:T(8,128)(2,1)S(1)} %collective-permute-done.sib, bf16[64,3072]{1,0:T(8,128)(2,1)S(1)} %collective-permute-done.1.far, ...), custom_call_target="tpu_custom_call" | custom-call | flops 4831838208 | bytes 18874368 | tf_op jit(solution)/shard_map/terms/pallas_call | solution.py:185
  34.2 1.0 %collective-permute-done.7.farsib = bf16[64,3072]{1,0:T(8,128)(2,1)S(1)} collective-permute-done((bf16[64,3072]{1,0:T(8,128)(2,1)S(1)}, bf16[64,3072]{1,0:T(8,128)(2,1)S(1)}, u32[]{:S(2)}, u32[]{:S(2)}) %collective-permute-start.7) | collective-permute-done | bytes 393248 | tf_op jit(solution)/shard_map/ppermute | solution.py:282
  35.2 8.7 %terms.3 = (bf16[2,32,3072]{2,1,0:T(8,128)(2,1)S(1)}, bf16[32,3072]{1,0:T(8,128)(2,1)S(1)}, bf16[32,3072]{1,0:T(8,128)(2,1)S(1)}, f32[32,3072]{1,0:T(8,128)S(1)}...) custom-call(s32[3]{0:T(128)S(1)} %pad_add_fusion.place_ref, ...), custom_call_target="tpu_custom_call" | custom-call | flops 4831838208 | bytes 18874368 | tf_op jit(solution)/shard_map/terms/pallas_call | solution.py:185
  43.9 0.6 collective-permute-start.8
  44.5 1.9 %collective-permute-start.12 = (bf16[2,32,3072]{2,1,0:T(8,128)(2,1)S(1)}, bf16[2,32,3072]{2,1,0:T(8,128)(2,1)S(1)}, u32[]{:S(2)}, u32[]{:S(2)}) collective-permute-start(bf16[2,32,3072]{2,1,0:T(8,128)(2,1)S(1)} %get-tuple-element.52), channel_id=1, source_target_pairs={{0,2},{1,3},{2,0},{3,1},{4,6},{5,7},{6,4},{7,5},{8,10},{9,11},{10,... | collective-permute-start | bytes 1179656 | tf_op jit(solution)/shard_map/ppermute | solution.py:282
  46.4 1.1 %input_columns.1.columns_ref = bf16[3072,256]{1,0:T(8,128)(2,1)S(1)} custom-call(s32[3]{0:T(128)S(1)} %pad_add_fusion.place_ref, bf16[2,32,3072]{2,1,0:T(8,128)(2,1)S(1)} %pair.2.near, bf16[2,32,3072]{2,1,0:T(8,128)(2,1)S(1)} %collective-permute-done.9.next_pair, bf16[32,3072]{1,0:T(8,128)(2,1)S(1)} %collective-permute-done.3.first.two, ...), custom_call_target="tpu_custom_call" | custom-call | bytes 3145728 | tf_op jit(solution)/shard_map/input_columns/pallas_call | solution.py:218
  47.5 2.7 %outer.3.refs_0_ = bf16[3072,6144]{1,0:T(8,128)(2,1)} custom-call(bf16[3072,256]{1,0:T(8,128)(2,1)S(1)} %input_columns.1.columns_ref, bf16[64,6144]{1,0:T(8,128)(2,1)S(1)} %get-tuple-element.33.own, bf16[64,6144]{1,0:T(8,128)(2,1)S(1)} %collective-permute-done.sib, bf16[64,3072]{1,0:T(8,128)(2,1)S(1)} %collective-permute-done.1.far, ...), custom_call_target="tpu_custom_call" | custom-call | flops 805306368 | bytes 3145728 | tf_op jit(solution)/shard_map/outer/pallas_call | solution.py:258
  50.2 0.7 collective-permute-done.8
  50.9 0.6 collective-permute-start.11
  51.6 2.6 %collective-permute-start.13 = (bf16[32,3072]{1,0:T(8,128)(2,1)S(1)}, bf16[32,3072]{1,0:T(8,128)(2,1)S(1)}, u32[]{:S(2)}, u32[]{:S(2)}) collective-permute-start(bf16[32,3072]{1,0:T(8,128)(2,1)S(1)} %add_convert_fusion.1), channel_id=1, source_target_pairs={{0,4},{1,5},{2,6},{3,7},{4,0},{5,1},{6,2},{7,3},{8,12},{9,13},{10,... | collective-permute-start | bytes 589832 | tf_op jit(solution)/shard_map/ppermute | solution.py:282
  54.1 7.6 %outer.4.refs_0_ = bf16[3072,6144]{1,0:T(8,128)(2,1)} custom-call(bf16[3072,256]{1,0:T(8,128)(2,1)S(1)} %input_columns.1.columns_ref, bf16[64,6144]{1,0:T(8,128)(2,1)S(1)} %get-tuple-element.33.own, bf16[64,6144]{1,0:T(8,128)(2,1)S(1)} %collective-permute-done.sib, bf16[64,3072]{1,0:T(8,128)(2,1)S(1)} %collective-permute-done.6.far, ...), custom_call_target="tpu_custom_call", output_to_operand_aliasing={{}: (5, {})} | custom-call | flops 4831838208 | bytes 18874368 | tf_op jit(solution)/shard_map/outer/pallas_call | solution.py:258
  61.8 0.8 %collective-permute-done.13 = bf16[32,3072]{1,0:T(8,128)(2,1)S(1)} collective-permute-done((bf16[32,3072]{1,0:T(8,128)(2,1)S(1)}, bf16[32,3072]{1,0:T(8,128)(2,1)S(1)}, u32[]{:S(2)}, u32[]{:S(2)}) %collective-permute-start.13) | collective-permute-done | bytes 196640 | tf_op jit(solution)/shard_map/ppermute | solution.py:282
  62.6 1.6 %collective-permute-start.14 = (bf16[32,3072]{1,0:T(8,128)(2,1)S(1)}, bf16[32,3072]{1,0:T(8,128)(2,1)S(1)}, u32[]{:S(2)}, u32[]{:S(2)}) collective-permute-start(bf16[32,3072]{1,0:T(8,128)(2,1)S(1)} %get-tuple-element.61), channel_id=1, source_target_pairs={{0,1},{1,0},{2,3},{3,2},{4,5},{5,4},{6,7},{7,6},{8,9},{9,8},{10,11... | collective-permute-start | bytes 589832 | tf_op jit(solution)/shard_map/ppermute | solution.py:282
  64.2 2.4 %collective-permute-start.15 = (bf16[32,3072]{1,0:T(8,128)(2,1)S(1)}, bf16[32,3072]{1,0:T(8,128)(2,1)S(1)}, u32[]{:S(2)}, u32[]{:S(2)}) collective-permute-start(bf16[32,3072]{1,0:T(8,128)(2,1)S(1)} %get-tuple-element.62), channel_id=1, source_target_pairs={{0,6},{1,7},{2,4},{3,5},{4,2},{5,3},{6,0},{7,1},{8,14},{9,15},{10,... | collective-permute-start | bytes 589832 | tf_op jit(solution)/shard_map/ppermute | solution.py:282
  66.6 6.6 %outer.5 = bf16[3072,6144]{1,0:T(8,128)(2,1)} custom-call(bf16[3072,256]{1,0:T(8,128)(2,1)S(1)} %input_columns.1.columns_ref, bf16[64,6144]{1,0:T(8,128)(2,1)S(1)} %get-tuple-element.33.own, bf16[64,6144]{1,0:T(8,128)(2,1)S(1)} %collective-permute-done.sib, bf16[64,3072]{1,0:T(8,128)(2,1)S(1)} %collective-permute-done.1.far, ...), custom_call_target="tpu_custom_call", output_to_operand_aliasing={{}: (5, {})} | custom-call | flops 4026531840 | bytes 15728640 | tf_op jit(solution)/shard_map/outer/pallas_call | solution.py:258
  73.2 0.8 %fusion.4 = bf16[32,3072]{1,0:T(8,128)(2,1)} fusion(f32[32,3072]{1,0:T(8,128)S(1)} %get-tuple-element.43, bf16[32,3072]{1,0:T(8,128)(2,1)S(1)} %collective-permute-done.15, bf16[32,3072]{1,0:T(8,128)(2,1)S(1)} %collective-permute-done.14, bf16[32,3072]{1,0:T(8,128)(2,1)S(1)} %collective-permute-done.13, bf16[2,32,3072]{2,1,0:T(8,128)(2,1)S(1)} %collective-permute-done.12), kind=kLoop, calls=%fused_computation.6 | loop fusion | flops 884736 | bytes 1376256 | tf_op jit(solution)/shard_map/convert_element_type | solution.py:335
  (23 shorter events, 1.6 us)
Async XLA Ops:
  3.7 16.9 %collective-permute-start.1 = (bf16[64,3072]{1,0:T(8,128)(2,1)S(1)}, bf16[64,3072]{1,0:T(8,128)(2,1)S(1)}, u32[]{:S(2)}, u32[]{:S(2)}) collective-permute-start(bf16[64,3072]{1,0:T(8,128)(2,1)S(1)} %get-tuple-element.34), channel_id=1, source_target_pairs={{0,16},{8,24},{16,0},{24,8},{1,17},{9,25},{17,1},{25,9},{2,18},{10... | collective-permute-start | bytes 1179656 | tf_op jit(solution)/shard_map/ppermute | solution.py:282
  6.8 18.0 %collective-permute-start = (bf16[64,6144]{1,0:T(8,128)(2,1)S(1)}, bf16[64,6144]{1,0:T(8,128)(2,1)S(1)}, u32[]{:S(2)}, u32[]{:S(2)}) collective-permute-start(bf16[64,6144]{1,0:T(8,128)(2,1)S(1)} %get-tuple-element.33.own), channel_id=1, source_target_pairs={{0,8},{8,0},{16,24},{24,16},{1,9},{9,1},{17,25},{25,17},{2,10},{10... | collective-permute-start | bytes 2359304 | tf_op jit(solution)/shard_map/ppermute | solution.py:282
  6.8 7.5 %collective-permute-start.2 = (bf16[32,3072]{1,0:T(8,128)(2,1)}, bf16[32,3072]{1,0:T(8,128)(2,1)S(1)}, u32[]{:S(2)}, u32[]{:S(2)}) collective-permute-start(bf16[32,3072]{1,0:T(8,128)(2,1)} %first.1), channel_id=1, source_target_pairs={{0,1},{1,0},{2,3},{3,2},{4,5},{5,4},{6,7},{7,6},{8,9},{9,8},{10,11... | collective-permute-start | bytes 589832 | tf_op jit(solution)/shard_map/ppermute | solution.py:282
  8.3 12.4 %collective-permute-start.3 = (bf16[32,3072]{1,0:T(8,128)(2,1)}, bf16[32,3072]{1,0:T(8,128)(2,1)S(1)}, u32[]{:S(2)}, u32[]{:S(2)}) collective-permute-start(bf16[32,3072]{1,0:T(8,128)(2,1)} %first.1), channel_id=1, source_target_pairs={{0,4},{1,5},{2,6},{3,7},{4,0},{5,1},{6,2},{7,3},{8,12},{9,13},{10,... | collective-permute-start | bytes 589832 | tf_op jit(solution)/shard_map/ppermute | solution.py:282
  14.3 0.9 %copy-start = (bf16[32,3072]{1,0:T(8,128)(2,1)S(1)}, bf16[32,3072]{1,0:T(8,128)(2,1)}, u32[]{:S(2)}) copy-start(bf16[32,3072]{1,0:T(8,128)(2,1)} %first.1) | copy-start | bytes 589828
  20.7 4.1 %collective-permute-start.4 = (bf16[64,3072]{1,0:T(8,128)(2,1)S(1)}, bf16[64,3072]{1,0:T(8,128)(2,1)S(1)}, u32[]{:S(2)}, u32[]{:S(2)}) collective-permute-start(bf16[64,3072]{1,0:T(8,128)(2,1)S(1)} %collective-permute-done.1.far), channel_id=1, source_target_pairs={{0,8},{8,0},{16,24},{24,16},{1,9},{9,1},{17,25},{25,17},{2,10},{10... | collective-permute-start | bytes 1179656 | tf_op jit(solution)/shard_map/ppermute | solution.py:282
  20.7 12.7 %collective-permute-start.6 = (bf16[64,3072]{1,0:T(8,128)(2,1)}, bf16[64,3072]{1,0:T(8,128)(2,1)S(1)}, u32[]{:S(2)}, u32[]{:S(2)}) collective-permute-start(bf16[64,3072]{1,0:T(8,128)(2,1)} %get-tuple-element.40), channel_id=1, source_target_pairs={{0,16},{8,24},{16,0},{24,8},{1,17},{9,25},{17,1},{25,9},{2,18},{10... | collective-permute-start | bytes 1179656 | tf_op jit(solution)/shard_map/ppermute | solution.py:282
  21.2 12.1 %collective-permute-start.5 = (bf16[32,3072]{1,0:T(8,128)(2,1)}, bf16[32,3072]{1,0:T(8,128)(2,1)S(1)}, u32[]{:S(2)}, u32[]{:S(2)}) collective-permute-start(bf16[32,3072]{1,0:T(8,128)(2,1)} %first.1), channel_id=1, source_target_pairs={{0,6},{1,7},{2,4},{3,5},{4,2},{5,3},{6,0},{7,1},{8,14},{9,15},{10,... | collective-permute-start | bytes 589832 | tf_op jit(solution)/shard_map/ppermute | solution.py:282
  33.4 1.8 %collective-permute-start.7 = (bf16[64,3072]{1,0:T(8,128)(2,1)S(1)}, bf16[64,3072]{1,0:T(8,128)(2,1)S(1)}, u32[]{:S(2)}, u32[]{:S(2)}) collective-permute-start(bf16[64,3072]{1,0:T(8,128)(2,1)S(1)} %collective-permute-done.6.far), channel_id=1, source_target_pairs={{0,8},{8,0},{16,24},{24,16},{1,9},{9,1},{17,25},{25,17},{2,10},{10... | collective-permute-start | bytes 1179656 | tf_op jit(solution)/shard_map/ppermute | solution.py:282
  33.5 12.9 %collective-permute-start.9 = (bf16[2,32,3072]{2,1,0:T(8,128)(2,1)S(1)}, bf16[2,32,3072]{2,1,0:T(8,128)(2,1)S(1)}, u32[]{:S(2)}, u32[]{:S(2)}) collective-permute-start(bf16[2,32,3072]{2,1,0:T(8,128)(2,1)S(1)} %pair.2.near), channel_id=1, source_target_pairs={{0,2},{1,3},{2,0},{3,1},{4,6},{5,7},{6,4},{7,5},{8,10},{9,11},{10,... | collective-permute-start | bytes 1179656 | tf_op jit(solution)/shard_map/ppermute | solution.py:282
  33.6 12.7 %collective-permute-start.10 = (bf16[2,32,3072]{2,1,0:T(8,128)(2,1)S(1)}, bf16[2,32,3072]{2,1,0:T(8,128)(2,1)S(1)}, u32[]{:S(2)}, u32[]{:S(2)}) collective-permute-start(bf16[2,32,3072]{2,1,0:T(8,128)(2,1)S(1)} %pair.3), channel_id=1, source_target_pairs={{0,1},{1,0},{2,3},{3,2},{4,5},{5,4},{6,7},{7,6},{8,9},{9,8},{10,11... | collective-permute-start | bytes 1179656 | tf_op jit(solution)/shard_map/ppermute | solution.py:282
  43.9 7.0 %collective-permute-start.8 = (bf16[32,3072]{1,0:T(8,128)(2,1)S(1)}, bf16[32,3072]{1,0:T(8,128)(2,1)S(1)}, u32[]{:S(2)}, u32[]{:S(2)}) collective-permute-start(bf16[32,3072]{1,0:T(8,128)(2,1)S(1)} %get-tuple-element.45), channel_id=1, source_target_pairs={{0,1},{1,0},{2,3},{3,2},{4,5},{5,4},{6,7},{7,6},{8,9},{9,8},{10,11... | collective-permute-start | bytes 589832 | tf_op jit(solution)/shard_map/ppermute | solution.py:282
  44.5 17.2 %collective-permute-start.12 = (bf16[2,32,3072]{2,1,0:T(8,128)(2,1)S(1)}, bf16[2,32,3072]{2,1,0:T(8,128)(2,1)S(1)}, u32[]{:S(2)}, u32[]{:S(2)}) collective-permute-start(bf16[2,32,3072]{2,1,0:T(8,128)(2,1)S(1)} %get-tuple-element.52), channel_id=1, source_target_pairs={{0,2},{1,3},{2,0},{3,1},{4,6},{5,7},{6,4},{7,5},{8,10},{9,11},{10,... | collective-permute-start | bytes 1179656 | tf_op jit(solution)/shard_map/ppermute | solution.py:282
  50.9 10.8 %collective-permute-start.11 = (bf16[32,3072]{1,0:T(8,128)(2,1)S(1)}, bf16[32,3072]{1,0:T(8,128)(2,1)S(1)}, u32[]{:S(2)}, u32[]{:S(2)}) collective-permute-start(bf16[32,3072]{1,0:T(8,128)(2,1)S(1)} %get-tuple-element.51), channel_id=1, source_target_pairs={{0,1},{1,0},{2,3},{3,2},{4,5},{5,4},{6,7},{7,6},{8,9},{9,8},{10,11... | collective-permute-start | bytes 589832 | tf_op jit(solution)/shard_map/ppermute | solution.py:282
  51.6 11.0 %collective-permute-start.13 = (bf16[32,3072]{1,0:T(8,128)(2,1)S(1)}, bf16[32,3072]{1,0:T(8,128)(2,1)S(1)}, u32[]{:S(2)}, u32[]{:S(2)}) collective-permute-start(bf16[32,3072]{1,0:T(8,128)(2,1)S(1)} %add_convert_fusion.1), channel_id=1, source_target_pairs={{0,4},{1,5},{2,6},{3,7},{4,0},{5,1},{6,2},{7,3},{8,12},{9,13},{10,... | collective-permute-start | bytes 589832 | tf_op jit(solution)/shard_map/ppermute | solution.py:282
  62.6 10.6 %collective-permute-start.14 = (bf16[32,3072]{1,0:T(8,128)(2,1)S(1)}, bf16[32,3072]{1,0:T(8,128)(2,1)S(1)}, u32[]{:S(2)}, u32[]{:S(2)}) collective-permute-start(bf16[32,3072]{1,0:T(8,128)(2,1)S(1)} %get-tuple-element.61), channel_id=1, source_target_pairs={{0,1},{1,0},{2,3},{3,2},{4,5},{5,4},{6,7},{7,6},{8,9},{9,8},{10,11... | collective-permute-start | bytes 589832 | tf_op jit(solution)/shard_map/ppermute | solution.py:282
  64.2 9.1 %collective-permute-start.15 = (bf16[32,3072]{1,0:T(8,128)(2,1)S(1)}, bf16[32,3072]{1,0:T(8,128)(2,1)S(1)}, u32[]{:S(2)}, u32[]{:S(2)}) collective-permute-start(bf16[32,3072]{1,0:T(8,128)(2,1)S(1)} %get-tuple-element.62), channel_id=1, source_target_pairs={{0,6},{1,7},{2,4},{3,5},{4,2},{5,3},{6,0},{7,1},{8,14},{9,15},{10,... | collective-permute-start | bytes 589832 | tf_op jit(solution)/shard_map/ppermute | solution.py:282

commit v4 on v3

--- a/solution.py
+++ b/solution.py
@@ -293,12 +293,13 @@
     along = functools.partial(swap, axis="row", size=4)
 
     *sent, own = hidden_parts(hidden_pre, upstream, starts, sizes)
-    sib = along(own, bits=1)
     far = [along(part, bits=2) for part in sent]
     crossed_own, two = across(layer_input, bits=1), across(layer_input, bits=4)
-    near = pair_of(layer_input, crossed_own)
-
-    far[0], near, two = tied(far[0], near, two)
+    crossed_own, two = tied(crossed_own, two)
+    own, near = tied(own, pair_of(layer_input, crossed_own))
+    sib = along(own, bits=1)
+
+    far[0], near = tied(far[0], near)
     source, far[0] = tied(layer_input, far[0])
     parts = [[own, sib, far[0], along(far[0], bits=1)]]
     three, next_pair = across(source, bits=6), across(near, bits=2)

time: 74.2 us -> 72.5 us (0.977)
  starting transfers between devices: 21.6 us -> 19.2 us
    ppermute x16, starting transfers between devices: 21.6 us -> 19.2 us  [swap(): return lax.ppermute(value, axis, [(n, n ^ bits) for n in range(size)])]
  transfers between devices with their start and end apart: 16 -> 16, of which waited for: 5 -> 6; matrix products, arithmetic and copies ran while one was open for 0% -> 0% of each run, Pallas kernels for 48% -> 53%
where the time goes in v4:
time: 72.5 us; the launch traced here: 72.4 us
  Pallas kernels  38.4 us (53%)
  starting transfers between devices  19.2 us (26%)
  waiting for transfers between devices  12.1 us (17%)
  other arithmetic  0.97 us (1%)
  local copies, waits for them, and re-layouts  0.93 us (1%)
  between operations  0.76 us (1%)
    ppermute x16, starting transfers between devices, swap(): return lax.ppermute(value, axis, [(n, n ^ bits) for n in range(size)])  19.2 us
    pallas_call x2, Pallas kernels, terms_part(): pl.pallas_call(functools.partial(terms_kernel, starts, n, first, last), i...  17.3 us
    pallas_call x3, Pallas kernels, outer_part(): pl.pallas_call(functools.partial(outer_kernel, start, offset, size, block...  16.9 us
    ppermute x16, waiting for transfers between devices, swap(): return lax.ppermute(value, axis, [(n, n ^ bits) for n in range(size)])  12.1 us
    pallas_call x1, Pallas kernels, hidden_parts(): pl.pallas_call(functools.partial(hidden_kernel, starts, sizes), in_specs=...  3.11 us
  transfers between devices with their start and end apart: 16, of which 6 were waited for; matrix products, arithmetic and copies ran while one was open for 0% of the time, Pallas kernels for 53%

profile of v4, /device:TPU:0, one launch (start us, length us, event | category | flops | bytes accessed | tf_op | source)
XLA Modules:
  0.0 72.4 jit_solution(9230744928619328322)
XLA Ops:
  0.6 4.1 %collective-permute-start.1 = (bf16[32,3072]{1,0:T(8,128)(2,1)}, bf16[32,3072]{1,0:T(8,128)(2,1)S(1)}, u32[]{:S(2)}, u32[]{:S(2)}) collective-permute-start(bf16[32,3072]{1,0:T(8,128)(2,1)} %first.1), channel_id=1, source_target_pairs={{0,4},{1,5},{2,6},{3,7},{4,0},{5,1},{6,2},{7,3},{8,12},{9,13},{10,... | collective-permute-start | bytes 589832 | tf_op jit(solution)/shard_map/ppermute | solution.py:282
  4.7 1.5 %collective-permute-start = (bf16[32,3072]{1,0:T(8,128)(2,1)}, bf16[32,3072]{1,0:T(8,128)(2,1)S(1)}, u32[]{:S(2)}, u32[]{:S(2)}) collective-permute-start(bf16[32,3072]{1,0:T(8,128)(2,1)} %first.1), channel_id=1, source_target_pairs={{0,1},{1,0},{2,3},{3,2},{4,5},{5,4},{6,7},{7,6},{8,9},{9,8},{10,11... | collective-permute-start | bytes 589832 | tf_op jit(solution)/shard_map/ppermute | solution.py:282
  6.2 3.1 %hidden_grad.1 = (bf16[64,3072]{1,0:T(8,128)(2,1)S(1)}, bf16[64,3072]{1,0:T(8,128)(2,1)}, bf16[64,6144]{1,0:T(8,128)(2,1)S(1)}) custom-call(bf16[64,6144]{1,0:T(8,128)(2,1)} %pre_hbm.1, bf16[64,6144]{1,0:T(8,128)(2,1)} %up_hbm.1), custom_call_target="tpu_custom_call" | custom-call | flops 7864320 | bytes 2359296 | tf_op jit(solution)/shard_map/hidden_grad/pallas_call | solution.py:80
  9.3 1.6 %collective-permute-start.3 = (bf16[64,3072]{1,0:T(8,128)(2,1)S(1)}, bf16[64,3072]{1,0:T(8,128)(2,1)S(1)}, u32[]{:S(2)}, u32[]{:S(2)}) collective-permute-start(bf16[64,3072]{1,0:T(8,128)(2,1)S(1)} %get-tuple-element.40), channel_id=1, source_target_pairs={{0,16},{8,24},{16,0},{24,8},{1,17},{9,25},{17,1},{25,9},{2,18},{10... | collective-permute-start | bytes 1179656 | tf_op jit(solution)/shard_map/ppermute | solution.py:282
  10.9 3.1 %collective-permute-done.1.first.two = bf16[32,3072]{1,0:T(8,128)(2,1)S(1)} collective-permute-done((bf16[32,3072]{1,0:T(8,128)(2,1)}, bf16[32,3072]{1,0:T(8,128)(2,1)S(1)}, u32[]{:S(2)}, u32[]{:S(2)}) %collective-permute-start.1) | collective-permute-done | bytes 196640 | tf_op jit(solution)/shard_map/ppermute | solution.py:282
  14.1 0.9 %copy-done = bf16[32,3072]{1,0:T(8,128)(2,1)S(1)} copy-done((bf16[32,3072]{1,0:T(8,128)(2,1)S(1)}, bf16[32,3072]{1,0:T(8,128)(2,1)}, u32[]{:S(2)}) %copy-start) | copy-done | bytes 196632
  15.1 4.6 %collective-permute-done.3.far = bf16[64,3072]{1,0:T(8,128)(2,1)S(1)} collective-permute-done((bf16[64,3072]{1,0:T(8,128)(2,1)S(1)}, bf16[64,3072]{1,0:T(8,128)(2,1)S(1)}, u32[]{:S(2)}, u32[]{:S(2)}) %collective-permute-start.3) | collective-permute-done | bytes 393248 | tf_op jit(solution)/shard_map/ppermute | solution.py:282
  19.7 1.5 %collective-permute-start.6 = (bf16[64,3072]{1,0:T(8,128)(2,1)}, bf16[64,3072]{1,0:T(8,128)(2,1)S(1)}, u32[]{:S(2)}, u32[]{:S(2)}) collective-permute-start(bf16[64,3072]{1,0:T(8,128)(2,1)} %get-tuple-element.46), channel_id=1, source_target_pairs={{0,16},{8,24},{16,0},{24,8},{1,17},{9,25},{17,1},{25,9},{2,18},{10... | collective-permute-start | bytes 1179656 | tf_op jit(solution)/shard_map/ppermute | solution.py:282
  21.3 1.4 %collective-permute-start.5 = (bf16[32,3072]{1,0:T(8,128)(2,1)}, bf16[32,3072]{1,0:T(8,128)(2,1)S(1)}, u32[]{:S(2)}, u32[]{:S(2)}) collective-permute-start(bf16[32,3072]{1,0:T(8,128)(2,1)} %first.1), channel_id=1, source_target_pairs={{0,6},{1,7},{2,4},{3,5},{4,2},{5,3},{6,0},{7,1},{8,14},{9,15},{10,... | collective-permute-start | bytes 589832 | tf_op jit(solution)/shard_map/ppermute | solution.py:282
  22.7 8.5 %terms.2.refs_0_ = f32[8,32,3072]{2,1,0:T(8,128)S(1)} custom-call(s32[3]{0:T(128)S(1)} %pad_add_fusion.place_ref, bf16[64,6144]{1,0:T(8,128)(2,1)S(1)} %get-tuple-element.38.own, bf16[64,6144]{1,0:T(8,128)(2,1)S(1)} %collective-permute-done.2.sib, bf16[64,3072]{1,0:T(8,128)(2,1)S(1)} %collective-permute-done.3.far, ...), custom_call_target="tpu_custom_call" | custom-call | flops 4831838208 | bytes 18874368 | tf_op jit(solution)/shard_map/terms/pallas_call | solution.py:185
  31.4 3.1 %collective-permute-start.9 = (bf16[2,32,3072]{2,1,0:T(8,128)(2,1)S(1)}, bf16[2,32,3072]{2,1,0:T(8,128)(2,1)S(1)}, u32[]{:S(2)}, u32[]{:S(2)}) collective-permute-start(bf16[2,32,3072]{2,1,0:T(8,128)(2,1)S(1)} %pair.2.near), channel_id=1, source_target_pairs={{0,2},{1,3},{2,0},{3,1},{4,6},{5,7},{6,4},{7,5},{8,10},{9,11},{10,... | collective-permute-start | bytes 1179656 | tf_op jit(solution)/shard_map/ppermute | solution.py:282
  34.5 0.5 collective-permute-start.10
  35.1 8.7 %terms.3 = (bf16[2,32,3072]{2,1,0:T(8,128)(2,1)S(1)}, bf16[32,3072]{1,0:T(8,128)(2,1)S(1)}, bf16[32,3072]{1,0:T(8,128)(2,1)S(1)}, f32[32,3072]{1,0:T(8,128)S(1)}...) custom-call(s32[3]{0:T(128)S(1)} %pad_add_fusion.place_ref, ...), custom_call_target="tpu_custom_call" | custom-call | flops 4831838208 | bytes 18874368 | tf_op jit(solution)/shard_map/terms/pallas_call | solution.py:185
  43.8 1.6 %collective-permute-start.8 = (bf16[32,3072]{1,0:T(8,128)(2,1)S(1)}, bf16[32,3072]{1,0:T(8,128)(2,1)S(1)}, u32[]{:S(2)}, u32[]{:S(2)}) collective-permute-start(bf16[32,3072]{1,0:T(8,128)(2,1)S(1)} %get-tuple-element.51), channel_id=1, source_target_pairs={{0,1},{1,0},{2,3},{3,2},{4,5},{5,4},{6,7},{7,6},{8,9},{9,8},{10,11... | collective-permute-start | bytes 589832 | tf_op jit(solution)/shard_map/ppermute | solution.py:282
  45.7 1.1 %input_columns.1.columns_ref = bf16[3072,256]{1,0:T(8,128)(2,1)S(1)} custom-call(s32[3]{0:T(128)S(1)} %pad_add_fusion.place_ref, bf16[2,32,3072]{2,1,0:T(8,128)(2,1)S(1)} %pair.2.near, bf16[2,32,3072]{2,1,0:T(8,128)(2,1)S(1)} %collective-permute-done.9.next_pair, bf16[32,3072]{1,0:T(8,128)(2,1)S(1)} %collective-permute-done.1.first.two, ...), custom_call_target="tpu_custom_call" | custom-call | bytes 3145728 | tf_op jit(solution)/shard_map/input_columns/pallas_call | solution.py:218
  46.8 2.6 %outer.3.refs_0_ = bf16[3072,6144]{1,0:T(8,128)(2,1)} custom-call(bf16[3072,256]{1,0:T(8,128)(2,1)S(1)} %input_columns.1.columns_ref, bf16[64,6144]{1,0:T(8,128)(2,1)S(1)} %get-tuple-element.38.own, bf16[64,6144]{1,0:T(8,128)(2,1)S(1)} %collective-permute-done.2.sib, bf16[64,3072]{1,0:T(8,128)(2,1)S(1)} %collective-permute-done.3.far, ...), custom_call_target="tpu_custom_call" | custom-call | flops 805306368 | bytes 3145728 | tf_op jit(solution)/shard_map/outer/pallas_call | solution.py:258
  49.5 1.1 %collective-permute-done.8 = bf16[32,3072]{1,0:T(8,128)(2,1)S(1)} collective-permute-done((bf16[32,3072]{1,0:T(8,128)(2,1)S(1)}, bf16[32,3072]{1,0:T(8,128)(2,1)S(1)}, u32[]{:S(2)}, u32[]{:S(2)}) %collective-permute-start.8) | collective-permute-done | bytes 196640 | tf_op jit(solution)/shard_map/ppermute | solution.py:282
  50.6 1.5 %collective-permute-start.11 = (bf16[32,3072]{1,0:T(8,128)(2,1)S(1)}, bf16[32,3072]{1,0:T(8,128)(2,1)S(1)}, u32[]{:S(2)}, u32[]{:S(2)}) collective-permute-start(bf16[32,3072]{1,0:T(8,128)(2,1)S(1)} %get-tuple-element.57), channel_id=1, source_target_pairs={{0,1},{1,0},{2,3},{3,2},{4,5},{5,4},{6,7},{7,6},{8,9},{9,8},{10,11... | collective-permute-start | bytes 589832 | tf_op jit(solution)/shard_map/ppermute | solution.py:282
  52.3 7.6 %outer.4.refs_0_ = bf16[3072,6144]{1,0:T(8,128)(2,1)} custom-call(bf16[3072,256]{1,0:T(8,128)(2,1)S(1)} %input_columns.1.columns_ref, bf16[64,6144]{1,0:T(8,128)(2,1)S(1)} %get-tuple-element.38.own, bf16[64,6144]{1,0:T(8,128)(2,1)S(1)} %collective-permute-done.2.sib, ...), custom_call_target="tpu_custom_call", output_to_operand_aliasing={{}: (5, {})} | custom-call | flops 4831838208 | bytes 18874368 | tf_op jit(solution)/shard_map/outer/pallas_call | solution.py:258
  59.9 2.9 %collective-permute-done.13 = bf16[32,3072]{1,0:T(8,128)(2,1)S(1)} collective-permute-done((bf16[32,3072]{1,0:T(8,128)(2,1)S(1)}, bf16[32,3072]{1,0:T(8,128)(2,1)S(1)}, u32[]{:S(2)}, u32[]{:S(2)}) %collective-permute-start.13) | collective-permute-done | bytes 196640 | tf_op jit(solution)/shard_map/ppermute | solution.py:282
  62.9 0.7 collective-permute-start.14
  63.5 1.4 %collective-permute-start.15 = (bf16[32,3072]{1,0:T(8,128)(2,1)S(1)}, bf16[32,3072]{1,0:T(8,128)(2,1)S(1)}, u32[]{:S(2)}, u32[]{:S(2)}) collective-permute-start(bf16[32,3072]{1,0:T(8,128)(2,1)S(1)} %get-tuple-element.68), channel_id=1, source_target_pairs={{0,6},{1,7},{2,4},{3,5},{4,2},{5,3},{6,0},{7,1},{8,14},{9,15},{10,... | collective-permute-start | bytes 589832 | tf_op jit(solution)/shard_map/ppermute | solution.py:282
  64.9 6.6 %outer.5 = bf16[3072,6144]{1,0:T(8,128)(2,1)} custom-call(bf16[3072,256]{1,0:T(8,128)(2,1)S(1)} %input_columns.1.columns_ref, bf16[64,6144]{1,0:T(8,128)(2,1)S(1)} %get-tuple-element.38.own, bf16[64,6144]{1,0:T(8,128)(2,1)S(1)} %collective-permute-done.2.sib, bf16[64,3072]{1,0:T(8,128)(2,1)S(1)} %collective-permute-done.3.far, ...), custom_call_target="tpu_custom_call", output_to_operand_aliasing={{}: (5, {})} | custom-call | flops 4026531840 | bytes 15728640 | tf_op jit(solution)/shard_map/outer/pallas_call | solution.py:258
  71.6 0.8 %fusion.4 = bf16[32,3072]{1,0:T(8,128)(2,1)} fusion(f32[32,3072]{1,0:T(8,128)S(1)} %get-tuple-element.49, bf16[32,3072]{1,0:T(8,128)(2,1)S(1)} %collective-permute-done.15, bf16[32,3072]{1,0:T(8,128)(2,1)S(1)} %collective-permute-done.14, bf16[32,3072]{1,0:T(8,128)(2,1)S(1)} %collective-permute-done.13, bf16[2,32,3072]{2,1,0:T(8,128)(2,1)S(1)} %collective-permute-done.12), kind=kLoop, calls=%fused_computation.6 | loop fusion | flops 884736 | bytes 1376256 | tf_op jit(solution)/shard_map/convert_element_type | solution.py:336
  (23 shorter events, 1.0 us)
Async XLA Ops:
  0.6 13.4 %collective-permute-start.1 = (bf16[32,3072]{1,0:T(8,128)(2,1)}, bf16[32,3072]{1,0:T(8,128)(2,1)S(1)}, u32[]{:S(2)}, u32[]{:S(2)}) collective-permute-start(bf16[32,3072]{1,0:T(8,128)(2,1)} %first.1), channel_id=1, source_target_pairs={{0,4},{1,5},{2,6},{3,7},{4,0},{5,1},{6,2},{7,3},{8,12},{9,13},{10,... | collective-permute-start | bytes 589832 | tf_op jit(solution)/shard_map/ppermute | solution.py:282
  4.7 9.3 %collective-permute-start = (bf16[32,3072]{1,0:T(8,128)(2,1)}, bf16[32,3072]{1,0:T(8,128)(2,1)S(1)}, u32[]{:S(2)}, u32[]{:S(2)}) collective-permute-start(bf16[32,3072]{1,0:T(8,128)(2,1)} %first.1), channel_id=1, source_target_pairs={{0,1},{1,0},{2,3},{3,2},{4,5},{5,4},{6,7},{7,6},{8,9},{9,8},{10,11... | collective-permute-start | bytes 589832 | tf_op jit(solution)/shard_map/ppermute | solution.py:282
  9.3 10.4 %collective-permute-start.3 = (bf16[64,3072]{1,0:T(8,128)(2,1)S(1)}, bf16[64,3072]{1,0:T(8,128)(2,1)S(1)}, u32[]{:S(2)}, u32[]{:S(2)}) collective-permute-start(bf16[64,3072]{1,0:T(8,128)(2,1)S(1)} %get-tuple-element.40), channel_id=1, source_target_pairs={{0,16},{8,24},{16,0},{24,8},{1,17},{9,25},{17,1},{25,9},{2,18},{10... | collective-permute-start | bytes 1179656 | tf_op jit(solution)/shard_map/ppermute | solution.py:282
  14.1 0.9 %copy-start = (bf16[32,3072]{1,0:T(8,128)(2,1)S(1)}, bf16[32,3072]{1,0:T(8,128)(2,1)}, u32[]{:S(2)}) copy-start(bf16[32,3072]{1,0:T(8,128)(2,1)} %first.1) | copy-start | bytes 589828
  15.0 7.7 %collective-permute-start.2 = (bf16[64,6144]{1,0:T(8,128)(2,1)S(1)}, bf16[64,6144]{1,0:T(8,128)(2,1)S(1)}, u32[]{:S(2)}, u32[]{:S(2)}) collective-permute-start(bf16[64,6144]{1,0:T(8,128)(2,1)S(1)} %get-tuple-element.38.own), channel_id=1, source_target_pairs={{0,8},{8,0},{16,24},{24,16},{1,9},{9,1},{17,25},{25,17},{2,10},{10... | collective-permute-start | bytes 2359304 | tf_op jit(solution)/shard_map/ppermute | solution.py:282
  19.7 3.0 %collective-permute-start.4 = (bf16[64,3072]{1,0:T(8,128)(2,1)S(1)}, bf16[64,3072]{1,0:T(8,128)(2,1)S(1)}, u32[]{:S(2)}, u32[]{:S(2)}) collective-permute-start(bf16[64,3072]{1,0:T(8,128)(2,1)S(1)} %collective-permute-done.3.far), channel_id=1, source_target_pairs={{0,8},{8,0},{16,24},{24,16},{1,9},{9,1},{17,25},{25,17},{2,10},{10... | collective-permute-start | bytes 1179656 | tf_op jit(solution)/shard_map/ppermute | solution.py:282
  19.7 11.7 %collective-permute-start.6 = (bf16[64,3072]{1,0:T(8,128)(2,1)}, bf16[64,3072]{1,0:T(8,128)(2,1)S(1)}, u32[]{:S(2)}, u32[]{:S(2)}) collective-permute-start(bf16[64,3072]{1,0:T(8,128)(2,1)} %get-tuple-element.46), channel_id=1, source_target_pairs={{0,16},{8,24},{16,0},{24,8},{1,17},{9,25},{17,1},{25,9},{2,18},{10... | collective-permute-start | bytes 1179656 | tf_op jit(solution)/shard_map/ppermute | solution.py:282
  21.3 9.9 %collective-permute-start.5 = (bf16[32,3072]{1,0:T(8,128)(2,1)}, bf16[32,3072]{1,0:T(8,128)(2,1)S(1)}, u32[]{:S(2)}, u32[]{:S(2)}) collective-permute-start(bf16[32,3072]{1,0:T(8,128)(2,1)} %first.1), channel_id=1, source_target_pairs={{0,6},{1,7},{2,4},{3,5},{4,2},{5,3},{6,0},{7,1},{8,14},{9,15},{10,... | collective-permute-start | bytes 589832 | tf_op jit(solution)/shard_map/ppermute | solution.py:282
  31.4 3.6 %collective-permute-start.7 = (bf16[64,3072]{1,0:T(8,128)(2,1)S(1)}, bf16[64,3072]{1,0:T(8,128)(2,1)S(1)}, u32[]{:S(2)}, u32[]{:S(2)}) collective-permute-start(bf16[64,3072]{1,0:T(8,128)(2,1)S(1)} %collective-permute-done.6.far), channel_id=1, source_target_pairs={{0,8},{8,0},{16,24},{24,16},{1,9},{9,1},{17,25},{25,17},{2,10},{10... | collective-permute-start | bytes 1179656 | tf_op jit(solution)/shard_map/ppermute | solution.py:282
  31.4 14.1 %collective-permute-start.9 = (bf16[2,32,3072]{2,1,0:T(8,128)(2,1)S(1)}, bf16[2,32,3072]{2,1,0:T(8,128)(2,1)S(1)}, u32[]{:S(2)}, u32[]{:S(2)}) collective-permute-start(bf16[2,32,3072]{2,1,0:T(8,128)(2,1)S(1)} %pair.2.near), channel_id=1, source_target_pairs={{0,2},{1,3},{2,0},{3,1},{4,6},{5,7},{6,4},{7,5},{8,10},{9,11},{10,... | collective-permute-start | bytes 1179656 | tf_op jit(solution)/shard_map/ppermute | solution.py:282
  34.5 11.2 %collective-permute-start.10 = (bf16[2,32,3072]{2,1,0:T(8,128)(2,1)S(1)}, bf16[2,32,3072]{2,1,0:T(8,128)(2,1)S(1)}, u32[]{:S(2)}, u32[]{:S(2)}) collective-permute-start(bf16[2,32,3072]{2,1,0:T(8,128)(2,1)S(1)} %pair.3), channel_id=1, source_target_pairs={{0,1},{1,0},{2,3},{3,2},{4,5},{5,4},{6,7},{7,6},{8,9},{9,8},{10,11... | collective-permute-start | bytes 1179656 | tf_op jit(solution)/shard_map/ppermute | solution.py:282
  43.8 6.8 %collective-permute-start.8 = (bf16[32,3072]{1,0:T(8,128)(2,1)S(1)}, bf16[32,3072]{1,0:T(8,128)(2,1)S(1)}, u32[]{:S(2)}, u32[]{:S(2)}) collective-permute-start(bf16[32,3072]{1,0:T(8,128)(2,1)S(1)} %get-tuple-element.51), channel_id=1, source_target_pairs={{0,1},{1,0},{2,3},{3,2},{4,5},{5,4},{6,7},{7,6},{8,9},{9,8},{10,11... | collective-permute-start | bytes 589832 | tf_op jit(solution)/shard_map/ppermute | solution.py:282
  45.4 14.5 %collective-permute-start.12 = (bf16[2,32,3072]{2,1,0:T(8,128)(2,1)S(1)}, bf16[2,32,3072]{2,1,0:T(8,128)(2,1)S(1)}, u32[]{:S(2)}, u32[]{:S(2)}) collective-permute-start(bf16[2,32,3072]{2,1,0:T(8,128)(2,1)S(1)} %get-tuple-element.58), channel_id=1, source_target_pairs={{0,2},{1,3},{2,0},{3,1},{4,6},{5,7},{6,4},{7,5},{8,10},{9,11},{10,... | collective-permute-start | bytes 1179656 | tf_op jit(solution)/shard_map/ppermute | solution.py:282
  50.6 9.3 %collective-permute-start.11 = (bf16[32,3072]{1,0:T(8,128)(2,1)S(1)}, bf16[32,3072]{1,0:T(8,128)(2,1)S(1)}, u32[]{:S(2)}, u32[]{:S(2)}) collective-permute-start(bf16[32,3072]{1,0:T(8,128)(2,1)S(1)} %get-tuple-element.57), channel_id=1, source_target_pairs={{0,1},{1,0},{2,3},{3,2},{4,5},{5,4},{6,7},{7,6},{8,9},{9,8},{10,11... | collective-permute-start | bytes 589832 | tf_op jit(solution)/shard_map/ppermute | solution.py:282
  52.1 10.7 %collective-permute-start.13 = (bf16[32,3072]{1,0:T(8,128)(2,1)S(1)}, bf16[32,3072]{1,0:T(8,128)(2,1)S(1)}, u32[]{:S(2)}, u32[]{:S(2)}) collective-permute-start(bf16[32,3072]{1,0:T(8,128)(2,1)S(1)} %add_convert_fusion.1), channel_id=1, source_target_pairs={{0,4},{1,5},{2,6},{3,7},{4,0},{5,1},{6,2},{7,3},{8,12},{9,13},{10,... | collective-permute-start | bytes 589832 | tf_op jit(solution)/shard_map/ppermute | solution.py:282
  62.9 8.7 %collective-permute-start.14 = (bf16[32,3072]{1,0:T(8,128)(2,1)S(1)}, bf16[32,3072]{1,0:T(8,128)(2,1)S(1)}, u32[]{:S(2)}, u32[]{:S(2)}) collective-permute-start(bf16[32,3072]{1,0:T(8,128)(2,1)S(1)} %get-tuple-element.67), channel_id=1, source_target_pairs={{0,1},{1,0},{2,3},{3,2},{4,5},{5,4},{6,7},{7,6},{8,9},{9,8},{10,11... | collective-permute-start | bytes 589832 | tf_op jit(solution)/shard_map/ppermute | solution.py:282
  63.5 8.0 %collective-permute-start.15 = (bf16[32,3072]{1,0:T(8,128)(2,1)S(1)}, bf16[32,3072]{1,0:T(8,128)(2,1)S(1)}, u32[]{:S(2)}, u32[]{:S(2)}) collective-permute-start(bf16[32,3072]{1,0:T(8,128)(2,1)S(1)} %get-tuple-element.68), channel_id=1, source_target_pairs={{0,6},{1,7},{2,4},{3,5},{4,2},{5,3},{6,0},{7,1},{8,14},{9,15},{10,... | collective-permute-start | bytes 589832 | tf_op jit(solution)/shard_map/ppermute | solution.py:282
